TPU v7x, 256 devices: a whole 4x4x8 slice. The times are simulated.
256 devices in a mesh: dp: 64 (over z, x, core), group: 4 (over y).
Axes of the slice: x: 4, y: 4, z: 8, core: 2. Of those that a mesh axis runs over, the one named last changes fastest.
Arguments:
- embeddings: bfloat16 [262144, 768], P(('dp', 'group')), may hold values from -200 to 200, as said below
- cluster_of: int32 [262144, 1], P(('dp', 'group')), may hold values from 0 to 127; in each aligned block of 1024 rows (0 to 1023, 1024 to 2047, ...) at most 16 rows name the same one
Outputs:
- nearest: float32 [262144], P(('dp', 'group'))
Inputs may be any that keep to these rules, and one draw needn't show every extreme that they name: `cluster_of`: among the 1024 rows of one device, at most 16 name one cluster, and in every draw some device has exactly 16 rows of one cluster. `embeddings`: no row is all zeros.
All inputs are finite; a program needn't handle non-finite values.
Results may differ from a plain program's by a relative error of at most 0.00076.
Values may be sent and summed in bfloat16 or wider, within the bound.
A program may use at most 64 MiB of HBM per device.

v0:
```python
import jax
import jax.numpy as jnp
from jax import lax
from jax.sharding import PartitionSpec as P

CLU_DP = 2


def passed_along(block, axis, distance):
    devices = range(lax.axis_size(axis))
    route = [((i - distance) % len(devices), i) for i in devices]
    return lax.ppermute(block, axis, route)


def tile_scores(own_rows, other_rows):
    return jnp.einsum("cmd,cnd->cmn", own_rows, other_rows, preferred_element_type=jnp.float32)


def live_rows(member_rows):
    return jnp.any(member_rows != 0, axis=2)


def on_device(embeddings, cluster_of):
    count_rows = embeddings.shape[0]
    feature_count = embeddings.shape[1]
    dp_count = lax.axis_size("dp")
    group_count = lax.axis_size("group")
    clusters = CLU_DP * dp_count
    capacity = 2 * count_rows // clusters
    widened = embeddings.astype(jnp.float32)
    square_sum = jnp.sum(widened * widened, axis=1, keepdims=True)
    unit_rows = (widened / jnp.sqrt(square_sum + 1e-06)).astype(jnp.bfloat16)
    labels = cluster_of[:, 0]
    onehot = (labels[:, None] == jnp.arange(clusters, dtype=jnp.int32)[None, :]).astype(jnp.int32)
    slot_rank = jnp.sum((jnp.cumsum(onehot, axis=0) - onehot) * onehot, axis=1)
    position = labels * capacity + slot_rank
    outgoing = (
        jnp.zeros((clusters * capacity, feature_count), jnp.bfloat16).at[position].set(unit_rows)
    )
    outgoing = outgoing.reshape(clusters, capacity, feature_count)
    own_block = lax.all_to_all(outgoing, "dp", split_axis=0, concat_axis=1, tiled=True)
    own_live = live_rows(own_block)
    member_count = own_block.shape[1]
    diagonal = jnp.eye(member_count, dtype=jnp.bool_)[None, :, :]
    scores = tile_scores(own_block, own_block)
    nearest_now = jnp.max(
        jnp.where(own_live[:, None, :] & jnp.logical_not(diagonal), scores, -1.0), axis=2
    )
    visitor = own_block
    for offset in range(1, group_count):
        visitor = passed_along(visitor, "group", 1)
        scores = tile_scores(own_block, visitor)
        visitor_live = live_rows(visitor)
        nearest_now = jnp.maximum(
            nearest_now, jnp.max(jnp.where(visitor_live[:, None, :], scores, -1.0), axis=2)
        )
    per_source = nearest_now.reshape(CLU_DP, dp_count, capacity)
    arrived = lax.all_to_all(per_source, "dp", split_axis=1, concat_axis=0, tiled=True)
    arrived = arrived.reshape(clusters * capacity)
    return arrived[position]


def solution(mesh):
    return jax.shard_map(
        on_device,
        mesh=mesh,
        in_specs=(P(("dp", "group"), None), P(("dp", "group"), None)),
        out_specs=P(("dp", "group")),
        check_vma=False,
    )
```

profile of v0, /device:TPU:1, one launch (start us, length us, event | category | flops | bytes accessed | tf_op | source)
XLA Modules:
  0.0 346.5 jit_solution(12889029604652203153)
XLA Ops:
  0.0 1.8 fusion.1
  1.8 0.8 copy.8
  2.6 0.2 fusion.9
  2.9 0.1 copy.9
  3.0 0.4 fusion.8
  3.4 7.2 %scatter_custom_fusion = bf16[2048,768]{1,0:T(8,128)(2,1)S(1)} fusion(s32[1024]{0:T(1024)S(1)} %bitcast.45, bf16[1024,768]{1,0:T(8,128)(2,1)} %param.2, f32[1024]{0:T(1024)S(1)} %add_sqrt_fusion, bf16[]{:T(256)} %constant.9.clone.1), kind=kCustom, calls=%fused_computation.16 | custom fusion | flops 2359296 | bytes 4722690 | tf_op jit(solution)/shard_map/scatter | solution.py:38
  10.6 85.6 %all_to_all.33 = bf16[128,16,768]{2,1,0:T(8,128)(2,1)S(1)} all-to-all(bf16[128,16,768]{2,1,0:T(8,128)(2,1)S(1)} %bitcast.35), channel_id=1, replica_groups=mesh['dp'=64,'group'=4] {'dp'}, dimensions={0} | all-to-all | bytes 6291456 | tf_op jit(solution)/shard_map/all_to_all | solution.py:41
  96.2 0.2 copy.11
  96.5 1.4 collective-permute-start
  97.8 68.2 %collective-permute-done = bf16[2,1024,768]{2,1,0:T(8,128)(2,1)S(1)} collective-permute-done((bf16[2,1024,768]{2,1,0:T(8,128)(2,1)S(1)}, bf16[2,1024,768]{2,1,0:T(8,128)(2,1)S(1)}, u32[]{:S(2)}, u32[]{:S(2)}) %collective-permute-start) | collective-permute-done | bytes 3145760 | tf_op jit(solution)/shard_map/ppermute | solution.py:12
  166.0 1.7 copy-done
  167.7 0.0 collective-permute-start.1
  167.7 1.3 fusion
  169.0 67.3 %collective-permute-done.1 = bf16[2,1024,768]{2,1,0:T(8,128)(2,1)} collective-permute-done((bf16[2,1024,768]{2,1,0:T(8,128)(2,1)S(1)}, bf16[2,1024,768]{2,1,0:T(8,128)(2,1)}, u32[]{:S(2)}, u32[]{:S(2)}) %collective-permute-start.1) | collective-permute-done | bytes 3145760 | tf_op jit(solution)/shard_map/ppermute | solution.py:12
  236.3 0.0 collective-permute-start.2
  236.3 2.4 compare_reduce_fusion.3
  238.7 0.1 and.15
  238.8 5.0 %select_reduce_fusion.3 = f32[2,1024]{1,0:T(2,128)S(1)} fusion(pred[1024,1024]{0,1:T(8,128)(4,1)} %fusion, pred[2,1024]{1,0:T(4,128)(4,1)S(1)} %and.15, bf16[2,1024,768]{2,1,0:T(8,128)(2,1)S(1)} %bitcast.37), kind=kOutput, calls=%fused_computation.5 | convolution fusion | flops 3227514880 | bytes 4204544 | tf_op jit(solution)/shard_map/cmd,cnd->cmn/dot_general | solution.py:16
  243.8 0.0 copy-done.1
  243.8 0.8 compare_reduce_fusion.2
  244.6 3.7 %select_reduce_fusion.2 = f32[2,1024]{1,0:T(2,128)S(1)} fusion(pred[2,1024]{1,0:T(4,128)(4,1)S(1)} %compare_reduce_fusion.2, bf16[2,1024,768]{2,1,0:T(8,128)(2,1)S(1)} %bitcast.38, bf16[2,1024,768]{2,1,0:T(8,128)(2,1)S(1)} %copy-done.1), kind=kOutput, calls=%fused_computation.4 | convolution fusion | flops 3225417728 | bytes 6301696 | tf_op jit(solution)/shard_map/cmd,cnd->cmn/dot_general | solution.py:16
  248.3 2.6 compare_reduce_fusion.1
  251.0 5.4 %select_reduce_fusion.1 = f32[2,1024]{1,0:T(2,128)S(1)} fusion(pred[2,1024]{1,0:T(4,128)(4,1)S(1)} %compare_reduce_fusion.1, bf16[2,1024,768]{2,1,0:T(8,128)(2,1)S(1)} %bitcast.39, bf16[2,1024,768]{2,1,0:T(8,128)(2,1)} %collective-permute-done.1), kind=kOutput, calls=%fused_computation.3 | convolution fusion | flops 3225417728 | bytes 6301696 | tf_op jit(solution)/shard_map/cmd,cnd->cmn/dot_general | solution.py:16
  256.3 47.8 %collective-permute-done.2 = bf16[2,1024,768]{2,1,0:T(8,128)(2,1)} collective-permute-done((bf16[2,1024,768]{2,1,0:T(8,128)(2,1)}, bf16[2,1024,768]{2,1,0:T(8,128)(2,1)}, u32[]{:S(2)}, u32[]{:S(2)}) %collective-permute-start.2) | collective-permute-done | bytes 3145760 | tf_op jit(solution)/shard_map/ppermute | solution.py:12
  304.2 2.6 compare_reduce_fusion
  306.8 5.4 %select_reduce_fusion = f32[2,1024]{1,0:T(2,128)S(1)} fusion(pred[2,1024]{1,0:T(4,128)(4,1)S(1)} %compare_reduce_fusion, bf16[2,1024,768]{2,1,0:T(8,128)(2,1)S(1)} %bitcast.40, bf16[2,1024,768]{2,1,0:T(8,128)(2,1)} %collective-permute-done.2), kind=kOutput, calls=%fused_computation.2 | convolution fusion | flops 3225417728 | bytes 6301696 | tf_op jit(solution)/shard_map/cmd,cnd->cmn/dot_general | solution.py:16
  312.2 0.1 max.20
  312.3 0.7 copy.12
  312.9 12.8 %all-to-all-start.1 = ((f32[2,64,16]{2,0,1:T(2,128)}), f32[2,64,16]{2,0,1:T(2,128)S(1)}, u32[]{:S(2)}, u32[]{:S(2)}) async-start(f32[2,64,16]{2,0,1:T(2,128)} %copy.12), calls=%async_computation.1 | async-start | bytes 131072 | tf_op jit(solution)/shard_map/all_to_all | solution.py:58
  325.7 10.1 %all-to-all-done.1 = f32[2,64,16]{2,0,1:T(2,128)S(1)} async-done(((f32[2,64,16]{2,0,1:T(2,128)}), f32[2,64,16]{2,0,1:T(2,128)S(1)}, u32[]{:S(2)}, u32[]{:S(2)}) %all-to-all-start.1) | async-done | bytes 8224 | tf_op jit(solution)/shard_map/all_to_all | solution.py:58
  335.8 0.1 reshape.55
  335.9 10.5 %gather_fusion = f32[1024]{0:T(1024)} fusion(f32[2048]{0:T(1024)S(1)} %reshape.55, s32[1024]{0:T(1024)S(1)} %broadcast_clamp_fusion), kind=kCustom, calls=%fused_computation | custom fusion | bytes 12288 | tf_op jit(solution)/shard_map/gather | solution.py:60
  (13 shorter events, 0.1 us)
Async XLA Ops:
  0.0 3.0 copy-start.2
  96.5 69.5 %collective-permute-start = (bf16[2,1024,768]{2,1,0:T(8,128)(2,1)S(1)}, bf16[2,1024,768]{2,1,0:T(8,128)(2,1)S(1)}, u32[]{:S(2)}, u32[]{:S(2)}) collective-permute-start(bf16[2,1024,768]{2,1,0:T(8,128)(2,1)S(1)} %bitcast.36), channel_id=1, source_target_pairs={{3,0},{0,1},{1,2},{2,3},{7,4},{4,5},{5,6},{6,7},{11,8},{8,9},{9,10... | collective-permute-start | bytes 9437192 | tf_op jit(solution)/shard_map/ppermute | solution.py:12
  166.0 1.7 copy-start
  167.7 68.6 %collective-permute-start.1 = (bf16[2,1024,768]{2,1,0:T(8,128)(2,1)S(1)}, bf16[2,1024,768]{2,1,0:T(8,128)(2,1)}, u32[]{:S(2)}, u32[]{:S(2)}) collective-permute-start(bf16[2,1024,768]{2,1,0:T(8,128)(2,1)S(1)} %collective-permute-done), channel_id=1, source_target_pairs={{3,0},{0,1},{1,2},{2,3},{7,4},{4,5},{5,6},{6,7},{11,8},{8,9},{9,10... | collective-permute-start | bytes 9437192 | tf_op jit(solution)/shard_map/ppermute | solution.py:12
  236.3 67.9 %collective-permute-start.2 = (bf16[2,1024,768]{2,1,0:T(8,128)(2,1)}, bf16[2,1024,768]{2,1,0:T(8,128)(2,1)}, u32[]{:S(2)}, u32[]{:S(2)}) collective-permute-start(bf16[2,1024,768]{2,1,0:T(8,128)(2,1)} %collective-permute-done.1), channel_id=1, source_target_pairs={{3,0},{0,1},{1,2},{2,3},{7,4},{4,5},{5,6},{6,7},{11,8},{8,9},{9,10... | collective-permute-start | bytes 9437192 | tf_op jit(solution)/shard_map/ppermute | solution.py:12
  238.8 5.1 %copy-start.1 = (bf16[2,1024,768]{2,1,0:T(8,128)(2,1)S(1)}, bf16[2,1024,768]{2,1,0:T(8,128)(2,1)}, u32[]{:S(2)}) copy-start(bf16[2,1024,768]{2,1,0:T(8,128)(2,1)} %copy-done) | copy-start | bytes 9437188
  312.9 22.9 %all-to-all-start.1 = ((f32[2,64,16]{2,0,1:T(2,128)}), f32[2,64,16]{2,0,1:T(2,128)S(1)}, u32[]{:S(2)}, u32[]{:S(2)}) async-start(f32[2,64,16]{2,0,1:T(2,128)} %copy.12), calls=%async_computation.1 | async-start | bytes 131072 | tf_op jit(solution)/shard_map/all_to_all | solution.py:58
where the time goes:
time: 347 us; the launch traced here: 346 us
  waiting for transfers between devices  193 us (56%)
  blocking collectives  85.6 us (25%)
  other arithmetic  19.4 us (6%)
  matrix products  19.4 us (6%)
  local copies, waits for them, and re-layouts  14.4 us (4%)
  starting transfers between devices  14.1 us (4%)
    ppermute x3, waiting for transfers between devices, passed_along(): return lax.ppermute(block, axis, route)  183 us
    all_to_all x1, blocking collectives, on_device(): lax.all_to_all(outgoing, 'dp', split_axis=0, concat_axis=1, tiled=True)  85.6 us
    dot_general x4, matrix products, tile_scores(): jnp.einsum('cmd,cnd->cmn', own_rows, other_rows, preferred_element_type=j...  19.4 us
    all_to_all x1, starting transfers between devices, on_device(): lax.all_to_all(per_source, 'dp', split_axis=1, concat_axis=0, tiled=True)  12.8 us
    gather x1, local copies, waits for them, and re-layouts, on_device(): return arrived[position]  10.5 us
    all_to_all x1, waiting for transfers between devices, on_device(): lax.all_to_all(per_source, 'dp', split_axis=1, concat_axis=0, tiled=True)  10.1 us
    reduce_or x4, other arithmetic, live_rows(): return jnp.any(member_rows != 0, axis=2)  8.43 us
    scatter x1, other arithmetic, on_device(): jnp.zeros((clusters * capacity, feature_count), jnp.bfloat16).at[position]  7.19 us
  transfers between devices with their start and end apart: 4, of which 4 were waited for; matrix products, arithmetic and copies ran while one was open for 6% of the time, Pallas kernels for 0%

commit v1 on v0

v1 whole, which is shorter than its diff:
```python
import functools

import jax
import jax.numpy as jnp
from jax import lax
from jax.experimental import pallas as pl
from jax.experimental.pallas import tpu as pltpu
from jax.sharding import PartitionSpec as P

MESH = pl.DeviceIdType.MESH
NZ, NX, NY = 8, 4, 4
CHIPS = NZ * NX * NY
CAP = 16
BLK = 256
PER = BLK // CAP
GROUPS = CHIPS // PER
EMPTY = 4.0
LOW = -1e30


def kernel(
    emb_ref, lab_ref, out_ref,
    unit, send, held, twin, acc, res, back, onehot,
    send_sem, recv_sem, fwd_send, fwd_recv, ret_send, ret_recv,
):
    dp = lax.axis_index("dp")
    y = lax.axis_index("group")
    z, x, core = dp // (2 * NX), (dp // 2) % NX, dp % 2
    rows = emb_ref.shape[0]

    def chip_at(r, sign):
        dz, dx, dy = r % NZ, r // (NZ * NY), (r // NZ) % NY
        tz, tx = (z + sign * dz + NZ) % NZ, (x + sign * dx + NX) % NX
        return ((tz * NX + tx) * 2 + core, (y + sign * dy + NY) % NY)

    sibling = ((z * NX + x) * 2 + 1 - core, y)

    barrier = pltpu.get_barrier_semaphore()

    @pl.loop(1, CHIPS)
    def _(r):
        pl.semaphore_signal(barrier, inc=1, device_id=chip_at(r, 1), device_id_type=MESH)

    pl.semaphore_signal(barrier, inc=1, device_id=sibling, device_id_type=MESH)

    @pl.loop(0, rows // BLK)
    def _(i):
        wide = emb_ref[pl.ds(i * BLK, BLK), :].astype(jnp.float32)
        total = jnp.sum(wide * wide, axis=1, keepdims=True)
        unit[pl.ds(i * BLK, BLK), :] = (wide * (1.0 / jnp.sqrt(total + 1e-06))).astype(jnp.bfloat16)

    label = lab_ref[...]
    far_z = (label % NZ - z + NZ) % NZ
    far_x = (label // (NZ * NY) - x + NX) % NX
    far_y = ((label // NZ) % NY - y + NY) % NY
    offset = far_z + NZ * (far_x * NY + far_y)
    hot = offset == lax.broadcasted_iota(jnp.int32, (CHIPS, rows), 0)
    onehot[...] = hot.astype(jnp.bfloat16)
    before = (
        lax.broadcasted_iota(jnp.int32, (rows, rows), 0)
        < lax.broadcasted_iota(jnp.int32, (rows, rows), 1)
    ).astype(jnp.bfloat16)
    earlier = jnp.dot(onehot[...], before, preferred_element_type=jnp.float32)
    rank = jnp.sum(jnp.where(hot, earlier, 0.0), axis=0, keepdims=True).astype(jnp.int32)
    position = offset * CAP + rank

    acc[...] = jnp.full_like(acc, -1.0)

    pl.semaphore_wait(barrier, CHIPS)

    def outgoing(r, g):
        at = pl.ds(pl.multiple_of(r * CAP, CAP), CAP)
        return pltpu.make_async_remote_copy(
            src_ref=send.at[at], dst_ref=held.at[at], send_sem=send_sem, recv_sem=recv_sem.at[g],
            device_id=chip_at(r, 1), device_id_type=MESH,
        )

    @pl.loop(0, GROUPS)
    def _(g):
        base = pl.multiple_of(g * BLK, BLK)
        pick = position == base + lax.broadcasted_iota(jnp.int32, (BLK, rows), 0)
        chosen = pick.astype(jnp.float32)
        filled = jnp.sum(chosen, axis=1, keepdims=True)
        block = jnp.dot(chosen.astype(jnp.bfloat16), unit[...], preferred_element_type=jnp.float32)
        lane = lax.broadcasted_iota(jnp.int32, (BLK, 128), 1)
        mark = jnp.where((lane == 0) & (filled == 0.0), EMPTY, 0.0)
        send[pl.ds(base, BLK), :128] = (block[:, :128] + mark).astype(jnp.bfloat16)
        send[pl.ds(base, BLK), 128:] = block[:, 128:].astype(jnp.bfloat16)

        @pl.loop(1 - jnp.minimum(g, 1), PER)
        def _(k):
            outgoing(g * PER + k, g).start()

    held[:CAP, :] = send[:CAP, :]

    def forward(g):
        at = pl.ds(pl.multiple_of(g * BLK, BLK), BLK)
        return pltpu.make_async_remote_copy(
            src_ref=held.at[at], dst_ref=twin.at[at], send_sem=fwd_send, recv_sem=fwd_recv.at[g],
            device_id=sibling, device_id_type=MESH,
        )

    def meet(others, j, i, same):
        at = pl.ds(pl.multiple_of(i * BLK, BLK), BLK)
        other = others[pl.ds(pl.multiple_of(j * BLK, BLK), BLK), :]
        score = lax.dot_general(
            other, held[at, :], (((1,), (1,)), ((), ())), preferred_element_type=jnp.float32
        )
        score = score + jnp.where(other[:, 0:1].astype(jnp.float32) > 2.0, LOW, 0.0)
        if same:
            one = lax.broadcasted_iota(jnp.int32, (BLK, BLK), 0)
            two = lax.broadcasted_iota(jnp.int32, (BLK, BLK), 1)
            score = jnp.where(one == two, LOW, score)
        best = jnp.max(score.reshape(BLK // 8, 8, BLK), axis=0)
        acc[:, at] = jnp.maximum(acc[:, at], best)

    def arrive(g, first):
        taken = PER - 1 if first else PER
        start = CAP if first else g * BLK
        at = pl.ds(start if first else pl.multiple_of(start, BLK), taken * CAP)
        pltpu.make_async_copy(held.at[at], held.at[at], recv_sem.at[g]).wait()

    arrive(0, True)
    forward(0).start()
    meet(held, 0, 0, True)

    @pl.loop(1, GROUPS)
    def _(g):
        arrive(g, False)
        forward(g).start()
        meet(held, g, g, True)

        @pl.loop(0, g)
        def _(i):
            meet(held, g, i, False)
            meet(held, i, g, False)

        @pl.loop(0, g - 1)
        def _(j):
            meet(twin, j, g, False)

        forward(g - 1).wait_recv()

        @pl.loop(0, g + 1)
        def _(i):
            meet(twin, g - 1, i, False)

    forward(GROUPS - 1).wait_recv()

    def returning(r):
        return pltpu.make_async_remote_copy(
            src_ref=res.at[r // 8], dst_ref=back.at[r], send_sem=ret_send, recv_sem=ret_recv,
            device_id=chip_at(r, -1), device_id_type=MESH,
        )

    for i in range(GROUPS):
        meet(twin, GROUPS - 1, i, False)
        best = jnp.max(acc[:, i * BLK:(i + 1) * BLK], axis=0, keepdims=True)
        res[2 * i] = best[:, :128]
        res[2 * i + 1] = best[:, 128:]

        @pl.loop(1 if i == 0 else 0, PER)
        def _(k):
            returning(i * PER + k).start()

    back[0] = res[0]
    pltpu.make_async_copy(back.at[pl.ds(1, CHIPS - 1)], back.at[pl.ds(1, CHIPS - 1)], ret_recv).wait()

    got = back[...].reshape(CHIPS, 128)
    high = got.astype(jnp.bfloat16)
    rest = got - high.astype(jnp.float32)
    mid = rest.astype(jnp.bfloat16)
    low = (rest - mid.astype(jnp.float32)).astype(jnp.bfloat16)
    spread = jnp.zeros((128, rows), jnp.float32)
    for part in (high, mid, low):
        spread += lax.dot_general(
            part, onehot[...], (((0,), (0,)), ((), ())), preferred_element_type=jnp.float32
        )
    place = (offset % 8) * CAP + rank
    chosen = place == lax.broadcasted_iota(jnp.int32, (128, rows), 0)
    out_ref[...] = jnp.sum(jnp.where(chosen, spread, 0.0), axis=0, keepdims=True)

    pltpu.make_async_copy(send.at[pl.ds(CAP, (CHIPS - 1) * CAP)], send.at[pl.ds(CAP, (CHIPS - 1) * CAP)], send_sem).wait()
    pltpu.make_async_copy(held, held, fwd_send).wait()
    pltpu.make_async_copy(back.at[pl.ds(1, CHIPS - 1)], back.at[pl.ds(1, CHIPS - 1)], ret_send).wait()


def on_device(embeddings, cluster_of):
    rows, features = embeddings.shape
    slots = CHIPS * CAP
    nearest = pl.pallas_call(
        kernel,
        out_shape=jax.ShapeDtypeStruct((1, rows), jnp.float32),
        in_specs=[pl.BlockSpec(memory_space=pltpu.VMEM)] * 2,
        out_specs=pl.BlockSpec(memory_space=pltpu.VMEM),
        scratch_shapes=[
            pltpu.VMEM((rows, features), jnp.bfloat16),
            pltpu.VMEM((slots, features), jnp.bfloat16),
            pltpu.VMEM((slots, features), jnp.bfloat16),
            pltpu.VMEM((slots, features), jnp.bfloat16),
            pltpu.VMEM((8, slots), jnp.float32),
            pltpu.VMEM((CHIPS // 8, 1, 128), jnp.float32),
            pltpu.VMEM((CHIPS, 1, 128), jnp.float32),
            pltpu.VMEM((CHIPS, rows), jnp.bfloat16),
            pltpu.SemaphoreType.DMA,
            pltpu.SemaphoreType.DMA((GROUPS,)),
            pltpu.SemaphoreType.DMA,
            pltpu.SemaphoreType.DMA((GROUPS,)),
            pltpu.SemaphoreType.DMA,
            pltpu.SemaphoreType.DMA,
        ],
        compiler_params=pltpu.CompilerParams(
            collective_id=0, has_side_effects=True, vmem_limit_bytes=48 << 20
        ),
        cost_estimate=pl.CostEstimate(
            flops=2 * slots * 2 * slots * features, bytes_accessed=2 * rows * features, transcendentals=0
        ),
    )(embeddings, cluster_of.reshape(1, rows))
    return nearest.reshape(rows)


def solution(mesh):
    return jax.shard_map(
        on_device,
        mesh=mesh,
        in_specs=(P(("dp", "group"), None), P(("dp", "group"), None)),
        out_specs=P(("dp", "group")),
        check_vma=False,
    )
```

time: 347 us -> 112 us (0.32)
  waiting for transfers between devices: 193 us -> 0 us
  Pallas kernels: 0 us -> 109 us
  blocking collectives: 85.6 us -> 0 us
  matrix products: 19.4 us -> 0 us
  other arithmetic: 19.4 us -> 0 us
  starting transfers between devices: 14.1 us -> 0 us
  local copies, waits for them, and re-layouts: 14.4 us -> 2.69 us
    ppermute x3 -> x0, waiting for transfers between devices: 183 us -> none  [passed_along(): return lax.ppermute(block, axis, route)]
    pallas_call x0 -> x1, Pallas kernels: none -> 109 us  [on_device(): pl.pallas_call(kernel, out_shape=jax.ShapeDtypeStruct((1, rows), jnp.floa...]
    all_to_all x1 -> x0, blocking collectives: 85.6 us -> none  [on_device(): lax.all_to_all(outgoing, 'dp', split_axis=0, concat_axis=1, tiled=True)]
    dot_general x4 -> x0, matrix products: 19.4 us -> none  [tile_scores(): jnp.einsum('cmd,cnd->cmn', own_rows, other_rows, preferred_element_type=j...]
    all_to_all x1 -> x0, starting transfers between devices: 12.8 us -> none  [on_device(): lax.all_to_all(per_source, 'dp', split_axis=1, concat_axis=0, tiled=True)]
    gather x1 -> x0, local copies, waits for them, and re-layouts: 10.5 us -> none  [on_device(): return arrived[position]]
    all_to_all x1 -> x0, waiting for transfers between devices: 10.1 us -> none  [on_device(): lax.all_to_all(per_source, 'dp', split_axis=1, concat_axis=0, tiled=True)]
    reduce_or x4 -> x0, other arithmetic: 8.43 us -> none  [live_rows(): return jnp.any(member_rows != 0, axis=2)]
  transfers between devices with their start and end apart: 4 -> 0, of which waited for: 4 -> 0; matrix products, arithmetic and copies ran while one was open for 6% -> 0% of each run, Pallas kernels for 0% -> 0%
where the time goes in v1:
time: 112 us; the launch traced here: 111 us
  Pallas kernels  109 us (97%)
  local copies, waits for them, and re-layouts  2.69 us (2%)
    pallas_call x1, Pallas kernels, on_device(): pl.pallas_call(kernel, out_shape=jax.ShapeDtypeStruct((1, rows), jnp.floa...  109 us
    unnamed x5, local copies, waits for them, and re-layouts  2.69 us

profile of v1, /device:TPU:1, one launch (start us, length us, event | category | flops | bytes accessed | tf_op | source)
XLA Modules:
  0.0 111.5 jit_solution(4318387484596213234)
XLA Ops:
  0.0 0.0 copy-start
  0.0 1.4 %copy-done = bf16[1024,768]{1,0:T(8,128)(2,1)S(1)} copy-done((bf16[1024,768]{1,0:T(8,128)(2,1)S(1)}, bf16[1024,768]{1,0:T(8,128)(2,1)}, u32[]{:S(2)}) %copy-start) | copy-done | bytes 1572888
  1.4 0.0 copy-start.1
  1.4 0.7 copy-done.1
  2.1 108.8 %shard_map.28 = f32[1,1024]{1,0:T(1,128)S(1)} custom-call(bf16[1024,768]{1,0:T(8,128)(2,1)S(1)} %copy-done, s32[1,1024]{1,0:T(1,128)S(1)} %bitcast.3), custom_call_target="tpu_custom_call" | custom-call | flops 12884901888 | bytes 1572864 | tf_op jit(solution)/shard_map/pallas_call | solution.py:191
  110.9 0.6 copy.4
Async XLA Ops:
  0.0 1.4 %copy-start = (bf16[1024,768]{1,0:T(8,128)(2,1)S(1)}, bf16[1024,768]{1,0:T(8,128)(2,1)}, u32[]{:S(2)}) copy-start(bf16[1024,768]{1,0:T(8,128)(2,1)} %emb_ref.1) | copy-start | bytes 4718596
  1.4 0.7 copy-start.1

commit v2 on v0

v2 whole, which is shorter than its diff:
```python
import jax
import jax.numpy as jnp
from jax import lax
from jax.experimental import pallas as pl
from jax.experimental.pallas import tpu as pltpu
from jax.sharding import PartitionSpec as P

MESH = pl.DeviceIdType.MESH
NZ, NX, NY = 8, 4, 4
PLANE = NX * NY
CHIPS = NZ * PLANE
CAP = 16
GRP = NZ * CAP
PAIR = 2 * GRP
BOTH = 2 * PAIR
PAIRS = PLANE // 2
EARLY = 4
EMPTY = 4.0
LOW = -1e30
LANES = 128


def kernel(
    emb_hbm, lab_hbm, out_ref,
    emb, lab, send, pool, acc, res, mid, back, onehot,
    emb_sem, lab_sem, send_sem, recv_sem, fwd_send, fwd_recv, one_send, one_recv, two_send, two_recv,
):
    dp = lax.axis_index("dp")
    y = lax.axis_index("group")
    z, x, core = dp // (2 * NX), (dp // 2) % NX, dp % 2
    rows = emb.shape[0]
    quarter = rows // 4

    def loading(i):
        at = pl.ds(i * quarter, quarter)
        return pltpu.make_async_copy(emb_hbm.at[at], emb.at[at], emb_sem.at[i])

    labels = pltpu.make_async_copy(lab_hbm, lab, lab_sem)
    labels.start()
    for i in range(4):
        loading(i).start()

    z_ahead = [((z + d) % NZ) * (2 * NX) + core for d in range(NZ)]
    z_behind = [((z + NZ - d) % NZ) * (2 * NX) + core for d in range(NZ)]

    def ahead(d, p):
        return (z_ahead[d] + ((x + p // NY) % NX) * 2, (y + p % NY) % NY)

    def plane_behind(p):
        return (z_behind[0] + ((x + NX - p // NY) % NX) * 2, (y + NY - p % NY) % NY)

    def column_behind(d):
        return (z_behind[d] + x * 2, y)

    sibling = ((z * NX + x) * 2 + 1 - core, y)

    barrier = pltpu.get_barrier_semaphore()

    def greet(d, p):
        pl.semaphore_signal(barrier, inc=1, device_id=ahead(d, p), device_id_type=MESH)

    for d in range(1, NZ):
        greet(d, 0)

    @pl.loop(1, PLANE)
    def _(p):
        for d in range(NZ):
            greet(d, p)

    pl.semaphore_signal(barrier, inc=1, device_id=sibling, device_id_type=MESH)

    labels.wait()
    label = lab[...]
    far_z = (label % NZ - z + NZ) % NZ
    far_x = (label // PLANE // 2 - x + NX) % NX
    far_y = ((label // NZ) % NY - y + NY) % NY
    plane = far_x * NY + far_y
    hot = far_z * PLANE + plane == lax.broadcasted_iota(jnp.int32, (CHIPS, rows), 0)
    ones = hot.astype(jnp.bfloat16)
    onehot[...] = ones
    row = lax.broadcasted_iota(jnp.int32, (LANES, 2 * LANES), 0)
    col = lax.broadcasted_iota(jnp.int32, (LANES, 2 * LANES), 1)
    before = ((row < col) | (col >= LANES)).astype(jnp.bfloat16)
    ranks = []
    carry = jnp.zeros((CHIPS, LANES), jnp.float32)
    for t in range(rows // LANES):
        at = slice(t * LANES, (t + 1) * LANES)
        both = jnp.dot(ones[:, at], before, preferred_element_type=jnp.float32)
        earlier = jnp.where(hot[:, at], both[:, :LANES] + carry, 0.0)
        carry = carry + both[:, LANES:]
        ranks.append(jnp.sum(earlier, axis=0, keepdims=True))
    rank = jnp.concatenate(ranks, axis=1).astype(jnp.int32)
    position = (plane * NZ + far_z) * CAP + rank

    acc[...] = jnp.full_like(acc, -1.0)

    for i in range(4):
        loading(i).wait()

    def dispatch(h):
        base = pl.multiple_of(h * PAIR, PAIR)
        pick = position == base + lax.broadcasted_iota(jnp.int32, (PAIR, rows), 0)
        chosen = jnp.where(pick, 1.0, 0.0)
        filled = jnp.sum(chosen, axis=1, keepdims=True)
        wide = jnp.dot(chosen.astype(jnp.bfloat16), emb[...], preferred_element_type=jnp.float32)
        total = jnp.sum(wide * wide, axis=1, keepdims=True)
        wide = wide * (1.0 / jnp.sqrt(total + 1e-06))
        lane = lax.broadcasted_iota(jnp.int32, (PAIR, LANES), 1)
        mark = jnp.where((lane == 0) & (filled == 0.0), EMPTY, 0.0)
        send[pl.ds(base, PAIR), :LANES] = (wide[:, :LANES] + mark).astype(jnp.bfloat16)
        send[pl.ds(base, PAIR), LANES:] = wide[:, LANES:].astype(jnp.bfloat16)

    def outgoing(d, p):
        src = pl.ds(pl.multiple_of(p * GRP + d * CAP, CAP), CAP)
        dst = pl.ds(pl.multiple_of((p // 2) * BOTH + (p % 2) * GRP + d * CAP, CAP), CAP)
        return pltpu.make_async_remote_copy(
            src_ref=send.at[src], dst_ref=pool.at[dst], send_sem=send_sem, recv_sem=recv_sem.at[p],
            device_id=ahead(d, p), device_id_type=MESH,
        )

    @pl.loop(0, EARLY)
    def _(h):
        dispatch(h)

    pl.semaphore_wait(barrier, CHIPS)

    pltpu.make_async_copy(send.at[pl.ds(0, CAP)], pool.at[pl.ds(0, CAP)], recv_sem.at[0]).start()
    for d in range(1, NZ):
        outgoing(d, 0).start()

    @pl.loop(1, 2 * EARLY)
    def _(p):
        for d in range(NZ):
            outgoing(d, p).start()

    @pl.loop(EARLY, PAIRS)
    def _(h):
        dispatch(h)
        for odd in range(2):
            for d in range(NZ):
                outgoing(d, 2 * h + odd).start()

    def mine(h, odd):
        return pl.ds(pl.multiple_of(h * BOTH + odd * GRP, GRP), GRP)

    def theirs(h, odd):
        return pl.ds(pl.multiple_of(h * BOTH + PAIR + odd * GRP, GRP), GRP)

    def forward(h, odd):
        g = 2 * h + odd
        return pltpu.make_async_remote_copy(
            src_ref=pool.at[mine(h, odd)], dst_ref=pool.at[theirs(h, odd)],
            send_sem=fwd_send, recv_sem=fwd_recv.at[g], device_id=sibling, device_id_type=MESH,
        )

    def arrive(h, odd):
        at = mine(h, odd)
        pltpu.make_async_copy(pool.at[at], pool.at[at], recv_sem.at[2 * h + odd]).wait()

    def meet(other, i, same):
        own = pool[pl.ds(pl.multiple_of(i * BOTH, BOTH), PAIR), :]
        score = lax.dot_general(other, own, (((1,), (1,)), ((), ())), preferred_element_type=jnp.float32)
        score = score + jnp.where(other[:, 0:1].astype(jnp.float32) > 2.0, LOW, 0.0)
        if same:
            one = lax.broadcasted_iota(jnp.int32, score.shape, 0)
            two = lax.broadcasted_iota(jnp.int32, score.shape, 1)
            score = jnp.where(one == two, LOW, score)
        best = jnp.max(score.reshape(score.shape[0] // 8, 8, PAIR), axis=0)
        at = pl.ds(pl.multiple_of(i * PAIR, PAIR), PAIR)
        acc[:, at] = jnp.maximum(acc[:, at], best)

    def whole(h):
        return pool[pl.ds(pl.multiple_of(h * BOTH, BOTH), BOTH), :]

    def newest(h, odd):
        return jnp.concatenate([pool[mine(h, odd), :], pool[theirs(h, odd), :]], axis=0)

    def even_step(h):
        arrive(h, 0)
        forward(h, 0).start()
        forward(h, 0).wait_recv()

        @pl.loop(0, h)
        def _(i):
            meet(newest(h, 0), i, False)

        arrive(h, 1)
        forward(h, 1).start()

        @pl.loop(0, h)
        def _(j):
            meet(whole(j), h, False)

        forward(h, 1).wait_recv()

    @pl.loop(0, PAIRS - 1)
    def _(h):
        even_step(h)

        @pl.loop(0, h)
        def _(i):
            meet(newest(h, 1), i, False)

        meet(whole(h), h, True)

    last = PAIRS - 1
    even_step(last)

    def in_plane(p):
        return pltpu.make_async_remote_copy(
            src_ref=res.at[p], dst_ref=mid.at[p], send_sem=one_send, recv_sem=one_recv,
            device_id=plane_behind(p), device_id_type=MESH,
        )

    def finish(i, first):
        best = jnp.max(acc[:, pl.ds(pl.multiple_of(i * PAIR, PAIR), PAIR)], axis=0, keepdims=True)
        for odd in range(2):
            res[2 * i + odd] = best[:, odd * LANES:(odd + 1) * LANES]
            if first and odd == 0:
                mid[0] = best[:, :LANES]
            else:
                in_plane(2 * i + odd).start()

    meet(newest(last, 1), 0, False)
    finish(0, True)

    @pl.loop(1, last)
    def _(i):
        meet(newest(last, 1), i, False)
        finish(i, False)

    meet(whole(last), last, True)
    finish(last, False)

    rest = pl.ds(1, PLANE - 1)
    pltpu.make_async_copy(mid.at[rest], mid.at[rest], one_recv).wait()
    for d in range(1, NZ):
        pltpu.make_async_remote_copy(
            src_ref=mid, dst_ref=back.at[pl.ds(d * PLANE, PLANE)], send_sem=two_send, recv_sem=two_recv,
            device_id=column_behind(d), device_id_type=MESH,
        ).start()
    back[:PLANE] = mid[...]
    far = pl.ds(PLANE, CHIPS - PLANE)
    pltpu.make_async_copy(back.at[far], back.at[far], two_recv).wait()

    got = back[...].reshape(CHIPS, LANES)
    high = got.astype(jnp.bfloat16)
    rest_of = got - high.astype(jnp.float32)
    middle = rest_of.astype(jnp.bfloat16)
    low = (rest_of - middle.astype(jnp.float32)).astype(jnp.bfloat16)
    spread = jnp.zeros((LANES, rows), jnp.float32)
    for part in (high, middle, low):
        spread += lax.dot_general(
            part, onehot[...], (((0,), (0,)), ((), ())), preferred_element_type=jnp.float32
        )
    place = far_z * CAP + rank
    chosen = place == lax.broadcasted_iota(jnp.int32, (LANES, rows), 0)
    out_ref[...] = jnp.sum(jnp.where(chosen, spread, 0.0), axis=0, keepdims=True)

    sent = pl.ds(CAP, (CHIPS - 1) * CAP)
    pltpu.make_async_copy(send.at[sent], send.at[sent], send_sem).wait()
    half = pl.ds(0, PLANE * GRP)
    pltpu.make_async_copy(pool.at[half], pool.at[half], fwd_send).wait()
    pltpu.make_async_copy(res.at[rest], res.at[rest], one_send).wait()
    pltpu.make_async_copy(back.at[far], back.at[far], two_send).wait()


def on_device(embeddings, cluster_of):
    rows, features = embeddings.shape
    slots = CHIPS * CAP
    nearest = pl.pallas_call(
        kernel,
        out_shape=jax.ShapeDtypeStruct((1, rows), jnp.float32),
        in_specs=[pl.BlockSpec(memory_space=pltpu.HBM)] * 2,
        out_specs=pl.BlockSpec(memory_space=pltpu.VMEM),
        scratch_shapes=[
            pltpu.VMEM((rows, features), jnp.bfloat16),
            pltpu.VMEM((1, rows), jnp.int32),
            pltpu.VMEM((slots, features), jnp.bfloat16),
            pltpu.VMEM((2 * slots, features), jnp.bfloat16),
            pltpu.VMEM((8, slots), jnp.float32),
            pltpu.VMEM((PLANE, 1, LANES), jnp.float32),
            pltpu.VMEM((PLANE, 1, LANES), jnp.float32),
            pltpu.VMEM((CHIPS, 1, LANES), jnp.float32),
            pltpu.VMEM((CHIPS, rows), jnp.bfloat16),
            pltpu.SemaphoreType.DMA((4,)),
            pltpu.SemaphoreType.DMA,
            pltpu.SemaphoreType.DMA,
            pltpu.SemaphoreType.DMA((PLANE,)),
            pltpu.SemaphoreType.DMA,
            pltpu.SemaphoreType.DMA((PLANE,)),
            pltpu.SemaphoreType.DMA,
            pltpu.SemaphoreType.DMA,
            pltpu.SemaphoreType.DMA,
            pltpu.SemaphoreType.DMA,
        ],
        compiler_params=pltpu.CompilerParams(
            collective_id=0, has_side_effects=True, vmem_limit_bytes=56 << 20
        ),
        cost_estimate=pl.CostEstimate(
            flops=2 * slots * 2 * slots * features, bytes_accessed=2 * rows * features, transcendentals=0
        ),
    )(embeddings, cluster_of.reshape(1, rows))
    return nearest.reshape(rows)


def solution(mesh):
    return jax.shard_map(
        on_device,
        mesh=mesh,
        in_specs=(P(("dp", "group"), None), P(("dp", "group"), None)),
        out_specs=P(("dp", "group")),
        check_vma=False,
    )
```

time: 347 us -> 103 us (0.30)
  waiting for transfers between devices: 193 us -> 0 us
  Pallas kernels: 0 us -> 102 us
  blocking collectives: 85.6 us -> 0 us
  matrix products: 19.4 us -> 0 us
  other arithmetic: 19.4 us -> 0 us
  starting transfers between devices: 14.1 us -> 0 us
  local copies, waits for them, and re-layouts: 14.4 us -> 1.28 us
    ppermute x3 -> x0, waiting for transfers between devices: 183 us -> none  [passed_along(): return lax.ppermute(block, axis, route)]
    pallas_call x0 -> x1, Pallas kernels: none -> 102 us  [on_device(): pl.pallas_call(kernel, out_shape=jax.ShapeDtypeStruct((1, rows), jnp.floa...]
    all_to_all x1 -> x0, blocking collectives: 85.6 us -> none  [on_device(): lax.all_to_all(outgoing, 'dp', split_axis=0, concat_axis=1, tiled=True)]
    dot_general x4 -> x0, matrix products: 19.4 us -> none  [tile_scores(): jnp.einsum('cmd,cnd->cmn', own_rows, other_rows, preferred_element_type=j...]
    all_to_all x1 -> x0, starting transfers between devices: 12.8 us -> none  [on_device(): lax.all_to_all(per_source, 'dp', split_axis=1, concat_axis=0, tiled=True)]
    gather x1 -> x0, local copies, waits for them, and re-layouts: 10.5 us -> none  [on_device(): return arrived[position]]
    all_to_all x1 -> x0, waiting for transfers between devices: 10.1 us -> none  [on_device(): lax.all_to_all(per_source, 'dp', split_axis=1, concat_axis=0, tiled=True)]
    reduce_or x4 -> x0, other arithmetic: 8.43 us -> none  [live_rows(): return jnp.any(member_rows != 0, axis=2)]
  transfers between devices with their start and end apart: 4 -> 0, of which waited for: 4 -> 0; matrix products, arithmetic and copies ran while one was open for 6% -> 0% of each run, Pallas kernels for 0% -> 0%
where the time goes in v2:
time: 103 us
  Pallas kernels  102 us (99%)
  local copies, waits for them, and re-layouts  1.28 us (1%)
    pallas_call x1, Pallas kernels, on_device(): pl.pallas_call(kernel, out_shape=jax.ShapeDtypeStruct((1, rows), jnp.floa...  102 us

profile of v2, /device:TPU:1, one launch (start us, length us, event | category | flops | bytes accessed | tf_op | source)
XLA Modules:
  0.0 103.3 jit_solution(3477199717460875406)
XLA Ops:
  0.0 102.0 %shard_map.28 = f32[1,1024]{1,0:T(1,128)} custom-call(bf16[1024,768]{1,0:T(8,128)(2,1)} %emb_hbm.1, s32[1,1024]{1,0:T(1,128)} %bitcast.3), custom_call_target="tpu_custom_call" | custom-call | flops 12884901888 | bytes 1572864 | tf_op jit(solution)/shard_map/pallas_call | solution.py:271
  102.0 1.3 %copy.4 = f32[1024]{0:T(1024)} copy(f32[1024]{0:T(1024)} %bitcast.2) | data formatting | bytes 8192

commit v3 on v2

--- a/solution.py
+++ b/solution.py
@@ -14,7 +14,7 @@
 PAIR = 2 * GRP
 BOTH = 2 * PAIR
 PAIRS = PLANE // 2
-EARLY = 4
+EARLY = 2
 EMPTY = 4.0
 LOW = -1e30
 LANES = 128
@@ -22,8 +22,8 @@
 
 def kernel(
     emb_hbm, lab_hbm, out_ref,
-    emb, lab, send, pool, acc, res, mid, back, onehot,
-    emb_sem, lab_sem, send_sem, recv_sem, fwd_send, fwd_recv, one_send, one_recv, two_send, two_recv,
+    emb, lab, send, pool, acc, res, back, onehot,
+    emb_sem, lab_sem, send_sem, recv_sem, fwd_send, fwd_recv, ret_send, ret_recv,
 ):
     dp = lax.axis_index("dp")
     y = lax.axis_index("group")
@@ -43,29 +43,28 @@
     z_ahead = [((z + d) % NZ) * (2 * NX) + core for d in range(NZ)]
     z_behind = [((z + NZ - d) % NZ) * (2 * NX) + core for d in range(NZ)]
 
-    def ahead(d, p):
+    def ahead(d, g):
+        p = PLANE - 1 - g
         return (z_ahead[d] + ((x + p // NY) % NX) * 2, (y + p % NY) % NY)
 
-    def plane_behind(p):
-        return (z_behind[0] + ((x + NX - p // NY) % NX) * 2, (y + NY - p % NY) % NY)
-
-    def column_behind(d):
-        return (z_behind[d] + x * 2, y)
+    def behind(d, g):
+        p = PLANE - 1 - g
+        return (z_behind[d] + ((x + NX - p // NY) % NX) * 2, (y + NY - p % NY) % NY)
 
     sibling = ((z * NX + x) * 2 + 1 - core, y)
 
     barrier = pltpu.get_barrier_semaphore()
 
-    def greet(d, p):
-        pl.semaphore_signal(barrier, inc=1, device_id=ahead(d, p), device_id_type=MESH)
+    def greet(d, g):
+        pl.semaphore_signal(barrier, inc=1, device_id=ahead(d, g), device_id_type=MESH)
+
+    @pl.loop(0, PLANE - 1)
+    def _(g):
+        for d in range(NZ):
+            greet(d, g)
 
     for d in range(1, NZ):
-        greet(d, 0)
-
-    @pl.loop(1, PLANE)
-    def _(p):
-        for d in range(NZ):
-            greet(d, p)
+        greet(d, PLANE - 1)
 
     pl.semaphore_signal(barrier, inc=1, device_id=sibling, device_id_type=MESH)
 
@@ -74,8 +73,8 @@
     far_z = (label % NZ - z + NZ) % NZ
     far_x = (label // PLANE // 2 - x + NX) % NX
     far_y = ((label // NZ) % NY - y + NY) % NY
-    plane = far_x * NY + far_y
-    hot = far_z * PLANE + plane == lax.broadcasted_iota(jnp.int32, (CHIPS, rows), 0)
+    chip = (PLANE - 1 - far_x * NY - far_y) * NZ + far_z
+    hot = chip == lax.broadcasted_iota(jnp.int32, (CHIPS, rows), 0)
     ones = hot.astype(jnp.bfloat16)
     onehot[...] = ones
     row = lax.broadcasted_iota(jnp.int32, (LANES, 2 * LANES), 0)
@@ -90,7 +89,7 @@
         carry = carry + both[:, LANES:]
         ranks.append(jnp.sum(earlier, axis=0, keepdims=True))
     rank = jnp.concatenate(ranks, axis=1).astype(jnp.int32)
-    position = (plane * NZ + far_z) * CAP + rank
+    position = chip * CAP + rank
 
     acc[...] = jnp.full_like(acc, -1.0)
 
@@ -110,13 +109,19 @@
         send[pl.ds(base, PAIR), :LANES] = (wide[:, :LANES] + mark).astype(jnp.bfloat16)
         send[pl.ds(base, PAIR), LANES:] = wide[:, LANES:].astype(jnp.bfloat16)
 
-    def outgoing(d, p):
-        src = pl.ds(pl.multiple_of(p * GRP + d * CAP, CAP), CAP)
-        dst = pl.ds(pl.multiple_of((p // 2) * BOTH + (p % 2) * GRP + d * CAP, CAP), CAP)
+    def outgoing(d, h, odd):
+        g = 2 * h + odd
+        src = pl.ds(pl.multiple_of(g * GRP + d * CAP, CAP), CAP)
+        dst = pl.ds(pl.multiple_of(h * BOTH + odd * GRP + d * CAP, CAP), CAP)
         return pltpu.make_async_remote_copy(
-            src_ref=send.at[src], dst_ref=pool.at[dst], send_sem=send_sem, recv_sem=recv_sem.at[p],
-            device_id=ahead(d, p), device_id_type=MESH,
+            src_ref=send.at[src], dst_ref=pool.at[dst], send_sem=send_sem, recv_sem=recv_sem.at[g],
+            device_id=ahead(d, g), device_id_type=MESH,
         )
+
+    def send_pair(h):
+        for odd in range(2):
+            for d in range(NZ):
+                outgoing(d, h, odd).start()
 
     @pl.loop(0, EARLY)
     def _(h):
@@ -124,21 +129,23 @@
 
     pl.semaphore_wait(barrier, CHIPS)
 
-    pltpu.make_async_copy(send.at[pl.ds(0, CAP)], pool.at[pl.ds(0, CAP)], recv_sem.at[0]).start()
-    for d in range(1, NZ):
-        outgoing(d, 0).start()
-
-    @pl.loop(1, 2 * EARLY)
-    def _(p):
-        for d in range(NZ):
-            outgoing(d, p).start()
-
-    @pl.loop(EARLY, PAIRS)
+    @pl.loop(0, EARLY)
+    def _(h):
+        send_pair(h)
+
+    @pl.loop(EARLY, PAIRS - 1)
     def _(h):
         dispatch(h)
-        for odd in range(2):
-            for d in range(NZ):
-                outgoing(d, 2 * h + odd).start()
+        send_pair(h)
+
+    dispatch(PAIRS - 1)
+    for d in range(NZ):
+        outgoing(d, PAIRS - 1, 0).start()
+    own_src = pl.ds((PLANE - 1) * GRP, CAP)
+    own_dst = pl.ds((PAIRS - 1) * BOTH + GRP, CAP)
+    pltpu.make_async_copy(send.at[own_src], pool.at[own_dst], recv_sem.at[PLANE - 1]).start()
+    for d in range(1, NZ):
+        outgoing(d, PAIRS - 1, 1).start()
 
     def mine(h, odd):
         return pl.ds(pl.multiple_of(h * BOTH + odd * GRP, GRP), GRP)
@@ -204,50 +211,50 @@
         meet(whole(h), h, True)
 
     last = PAIRS - 1
-    even_step(last)
-
-    def in_plane(p):
+
+    def returning(d, g):
         return pltpu.make_async_remote_copy(
-            src_ref=res.at[p], dst_ref=mid.at[p], send_sem=one_send, recv_sem=one_recv,
-            device_id=plane_behind(p), device_id_type=MESH,
+            src_ref=res.at[g], dst_ref=back.at[g * NZ + d], send_sem=ret_send, recv_sem=ret_recv,
+            device_id=behind(d, g), device_id_type=MESH,
         )
 
-    def finish(i, first):
-        best = jnp.max(acc[:, pl.ds(pl.multiple_of(i * PAIR, PAIR), PAIR)], axis=0, keepdims=True)
+    def finish(i):
+        best = jnp.max(acc[:, i * PAIR:(i + 1) * PAIR], axis=0, keepdims=True)
         for odd in range(2):
-            res[2 * i + odd] = best[:, odd * LANES:(odd + 1) * LANES]
-            if first and odd == 0:
-                mid[0] = best[:, :LANES]
-            else:
-                in_plane(2 * i + odd).start()
-
-    meet(newest(last, 1), 0, False)
-    finish(0, True)
-
-    @pl.loop(1, last)
+            g = 2 * i + odd
+            res[g] = best[:, odd * LANES:(odd + 1) * LANES]
+            for d in range(NZ):
+                if g == PLANE - 1 and d == 0:
+                    pltpu.make_async_copy(res.at[g], back.at[g * NZ], ret_recv).start()
+                else:
+                    returning(d, g).start()
+
+    arrive(last, 0)
+    forward(last, 0).start()
+    forward(last, 0).wait_recv()
+
+    @pl.loop(0, last)
     def _(i):
+        meet(newest(last, 0), i, False)
+
+    arrive(last, 1)
+    forward(last, 1).start()
+    for j in range(last):
+        meet(whole(j), last, False)
+    forward(last, 1).wait_recv()
+    for i in range(last):
         meet(newest(last, 1), i, False)
-        finish(i, False)
-
+        finish(i)
     meet(whole(last), last, True)
-    finish(last, False)
-
-    rest = pl.ds(1, PLANE - 1)
-    pltpu.make_async_copy(mid.at[rest], mid.at[rest], one_recv).wait()
-    for d in range(1, NZ):
-        pltpu.make_async_remote_copy(
-            src_ref=mid, dst_ref=back.at[pl.ds(d * PLANE, PLANE)], send_sem=two_send, recv_sem=two_recv,
-            device_id=column_behind(d), device_id_type=MESH,
-        ).start()
-    back[:PLANE] = mid[...]
-    far = pl.ds(PLANE, CHIPS - PLANE)
-    pltpu.make_async_copy(back.at[far], back.at[far], two_recv).wait()
+    finish(last)
+
+    pltpu.make_async_copy(back, back, ret_recv).wait()
 
     got = back[...].reshape(CHIPS, LANES)
     high = got.astype(jnp.bfloat16)
-    rest_of = got - high.astype(jnp.float32)
-    middle = rest_of.astype(jnp.bfloat16)
-    low = (rest_of - middle.astype(jnp.float32)).astype(jnp.bfloat16)
+    rest = got - high.astype(jnp.float32)
+    middle = rest.astype(jnp.bfloat16)
+    low = (rest - middle.astype(jnp.float32)).astype(jnp.bfloat16)
     spread = jnp.zeros((LANES, rows), jnp.float32)
     for part in (high, middle, low):
         spread += lax.dot_general(
@@ -261,8 +268,8 @@
     pltpu.make_async_copy(send.at[sent], send.at[sent], send_sem).wait()
     half = pl.ds(0, PLANE * GRP)
     pltpu.make_async_copy(pool.at[half], pool.at[half], fwd_send).wait()
-    pltpu.make_async_copy(res.at[rest], res.at[rest], one_send).wait()
-    pltpu.make_async_copy(back.at[far], back.at[far], two_send).wait()
+    others = pl.ds(0, CHIPS - 1)
+    pltpu.make_async_copy(back.at[others], back.at[others], ret_send).wait()
 
 
 def on_device(embeddings, cluster_of):
@@ -280,7 +287,6 @@
             pltpu.VMEM((2 * slots, features), jnp.bfloat16),
             pltpu.VMEM((8, slots), jnp.float32),
             pltpu.VMEM((PLANE, 1, LANES), jnp.float32),
-            pltpu.VMEM((PLANE, 1, LANES), jnp.float32),
             pltpu.VMEM((CHIPS, 1, LANES), jnp.float32),
             pltpu.VMEM((CHIPS, rows), jnp.bfloat16),
             pltpu.SemaphoreType.DMA((4,)),
@@ -289,8 +295,6 @@
             pltpu.SemaphoreType.DMA((PLANE,)),
             pltpu.SemaphoreType.DMA,
             pltpu.SemaphoreType.DMA((PLANE,)),
-            pltpu.SemaphoreType.DMA,
-            pltpu.SemaphoreType.DMA,
             pltpu.SemaphoreType.DMA,
             pltpu.SemaphoreType.DMA,
         ],

time: 103 us -> 99.5 us (0.966)
  Pallas kernels: 102 us -> 98.1 us
    pallas_call x1, Pallas kernels: 102 us -> 98.1 us  [on_device(): pl.pallas_call(kernel, out_shape=jax.ShapeDtypeStruct((1, rows), jnp.floa...]
where the time goes in v3:
time: 99.5 us; the launch traced here: 99.4 us
  Pallas kernels  98.1 us (99%)
  local copies, waits for them, and re-layouts  1.28 us (1%)
    pallas_call x1, Pallas kernels, on_device(): pl.pallas_call(kernel, out_shape=jax.ShapeDtypeStruct((1, rows), jnp.floa...  98.1 us

profile of v3, /device:TPU:1, one launch (start us, length us, event | category | flops | bytes accessed | tf_op | source)
XLA Modules:
  0.0 99.4 jit_solution(12871639114364235765)
XLA Ops:
  0.0 98.1 %shard_map.28 = f32[1,1024]{1,0:T(1,128)} custom-call(bf16[1024,768]{1,0:T(8,128)(2,1)} %emb_hbm.1, s32[1,1024]{1,0:T(1,128)} %bitcast.3), custom_call_target="tpu_custom_call" | custom-call | flops 12884901888 | bytes 1572864 | tf_op jit(solution)/shard_map/pallas_call | solution.py:278
  98.1 1.3 %copy.4 = f32[1024]{0:T(1024)} copy(f32[1024]{0:T(1024)} %bitcast.2) | data formatting | bytes 8192

commit v4 on v3

--- a/solution.py
+++ b/solution.py
@@ -15,15 +15,26 @@
 BOTH = 2 * PAIR
 PAIRS = PLANE // 2
 EARLY = 2
+REACH = 3
 EMPTY = 4.0
 LOW = -1e30
 LANES = 128
 
 
+def hops(d, g):
+    p = PLANE - 1 - g
+    return sum(min(a, n - a) for a, n in ((d, NZ), (p // NY, NX), (p % NY, NY)))
+
+
+OFFSETS = [(d, g) for g in range(PLANE) for d in range(NZ) if hops(d, g)]
+NEAR = [o for o in OFFSETS if hops(*o) <= REACH]
+FAR = [o for o in OFFSETS if hops(*o) > REACH]
+
+
 def kernel(
-    emb_hbm, lab_hbm, out_ref,
-    emb, lab, send, pool, acc, res, back, onehot,
-    emb_sem, lab_sem, send_sem, recv_sem, fwd_send, fwd_recv, ret_send, ret_recv,
+    emb_hbm, lab_ref, out_ref,
+    emb, send, pool, acc, res, back, onehot,
+    emb_sem, near_sem, far_sem, send_sem, recv_sem, fwd_send, fwd_recv, ret_send, ret_recv,
 ):
     dp = lax.axis_index("dp")
     y = lax.axis_index("group")
@@ -35,41 +46,40 @@
         at = pl.ds(i * quarter, quarter)
         return pltpu.make_async_copy(emb_hbm.at[at], emb.at[at], emb_sem.at[i])
 
-    labels = pltpu.make_async_copy(lab_hbm, lab, lab_sem)
-    labels.start()
     for i in range(4):
         loading(i).start()
 
     z_ahead = [((z + d) % NZ) * (2 * NX) + core for d in range(NZ)]
     z_behind = [((z + NZ - d) % NZ) * (2 * NX) + core for d in range(NZ)]
 
+    x_ahead = [((x + d) % NX) * 2 for d in range(NX)]
+    y_ahead = [(y + d) % NY for d in range(NY)]
+
     def ahead(d, g):
         p = PLANE - 1 - g
-        return (z_ahead[d] + ((x + p // NY) % NX) * 2, (y + p % NY) % NY)
+        return (z_ahead[d] + x_ahead[p // NY], y_ahead[p % NY])
 
     def behind(d, g):
         p = PLANE - 1 - g
-        return (z_behind[d] + ((x + NX - p // NY) % NX) * 2, (y + NY - p % NY) % NY)
+        return (z_behind[d] + x_ahead[-(p // NY)], y_ahead[-(p % NY)])
 
     sibling = ((z * NX + x) * 2 + 1 - core, y)
 
     barrier = pltpu.get_barrier_semaphore()
 
-    def greet(d, g):
-        pl.semaphore_signal(barrier, inc=1, device_id=ahead(d, g), device_id_type=MESH)
-
-    @pl.loop(0, PLANE - 1)
-    def _(g):
-        for d in range(NZ):
-            greet(d, g)
-
-    for d in range(1, NZ):
-        greet(d, PLANE - 1)
+    def greet(d, g, counter):
+        chip, along = ahead(d, g)
+        pl.semaphore_signal(
+            barrier, inc=1, device_id=(chip - core + counter, along), device_id_type=MESH
+        )
 
     pl.semaphore_signal(barrier, inc=1, device_id=sibling, device_id_type=MESH)
-
-    labels.wait()
-    label = lab[...]
+    for offset in FAR:
+        greet(*offset, 1)
+    for offset in NEAR:
+        greet(*offset, 0)
+
+    label = lab_ref[...]
     far_z = (label % NZ - z + NZ) % NZ
     far_x = (label // PLANE // 2 - x + NX) % NX
     far_y = ((label // NZ) % NY - y + NY) % NY
@@ -97,7 +107,7 @@
         loading(i).wait()
 
     def dispatch(h):
-        base = pl.multiple_of(h * PAIR, PAIR)
+        base = h * PAIR
         pick = position == base + lax.broadcasted_iota(jnp.int32, (PAIR, rows), 0)
         chosen = jnp.where(pick, 1.0, 0.0)
         filled = jnp.sum(chosen, axis=1, keepdims=True)
@@ -109,43 +119,52 @@
         send[pl.ds(base, PAIR), :LANES] = (wide[:, :LANES] + mark).astype(jnp.bfloat16)
         send[pl.ds(base, PAIR), LANES:] = wide[:, LANES:].astype(jnp.bfloat16)
 
-    def outgoing(d, h, odd):
-        g = 2 * h + odd
-        src = pl.ds(pl.multiple_of(g * GRP + d * CAP, CAP), CAP)
-        dst = pl.ds(pl.multiple_of(h * BOTH + odd * GRP + d * CAP, CAP), CAP)
+    def outgoing(d, g):
+        src = pl.ds(g * GRP + d * CAP, CAP)
+        dst = pl.ds((g // 2) * BOTH + (g % 2) * GRP + d * CAP, CAP)
         return pltpu.make_async_remote_copy(
             src_ref=send.at[src], dst_ref=pool.at[dst], send_sem=send_sem, recv_sem=recv_sem.at[g],
             device_id=ahead(d, g), device_id_type=MESH,
         )
 
-    def send_pair(h):
-        for odd in range(2):
-            for d in range(NZ):
-                outgoing(d, h, odd).start()
-
-    @pl.loop(0, EARLY)
-    def _(h):
+    def send_near(h):
+        for d, g in NEAR:
+            if g // 2 == h:
+                outgoing(d, g).start()
+
+    for h in range(EARLY):
         dispatch(h)
 
-    pl.semaphore_wait(barrier, CHIPS)
-
-    @pl.loop(0, EARLY)
-    def _(h):
-        send_pair(h)
-
-    @pl.loop(EARLY, PAIRS - 1)
-    def _(h):
+    @pl.when(core == 0)
+    def _():
+        pl.semaphore_wait(barrier, 2 * len(NEAR) + 1)
+        pl.semaphore_signal(near_sem, inc=1, device_id=sibling, device_id_type=MESH)
+
+    @pl.when(core == 1)
+    def _():
+        pl.semaphore_wait(near_sem, 1)
+
+    for h in range(EARLY):
+        send_near(h)
+    for h in range(EARLY, PAIRS):
         dispatch(h)
-        send_pair(h)
-
-    dispatch(PAIRS - 1)
-    for d in range(NZ):
-        outgoing(d, PAIRS - 1, 0).start()
+        send_near(h)
+
     own_src = pl.ds((PLANE - 1) * GRP, CAP)
     own_dst = pl.ds((PAIRS - 1) * BOTH + GRP, CAP)
     pltpu.make_async_copy(send.at[own_src], pool.at[own_dst], recv_sem.at[PLANE - 1]).start()
-    for d in range(1, NZ):
-        outgoing(d, PAIRS - 1, 1).start()
+
+    @pl.when(core == 1)
+    def _():
+        pl.semaphore_wait(barrier, 2 * len(FAR) + 1)
+        pl.semaphore_signal(far_sem, inc=1, device_id=sibling, device_id_type=MESH)
+
+    @pl.when(core == 0)
+    def _():
+        pl.semaphore_wait(far_sem, 1)
+
+    for d, g in FAR:
+        outgoing(d, g).start()
 
     def mine(h, odd):
         return pl.ds(pl.multiple_of(h * BOTH + odd * GRP, GRP), GRP)
@@ -182,31 +201,26 @@
     def newest(h, odd):
         return jnp.concatenate([pool[mine(h, odd), :], pool[theirs(h, odd), :]], axis=0)
 
-    def even_step(h):
-        arrive(h, 0)
-        forward(h, 0).start()
-        forward(h, 0).wait_recv()
-
-        @pl.loop(0, h)
-        def _(i):
-            meet(newest(h, 0), i, False)
-
-        arrive(h, 1)
-        forward(h, 1).start()
-
-        @pl.loop(0, h)
-        def _(j):
-            meet(whole(j), h, False)
-
-        forward(h, 1).wait_recv()
+    def cross(h, i):
+        meet(whole(i), h, False)
+        meet(whole(h), i, False)
 
     @pl.loop(0, PAIRS - 1)
     def _(h):
-        even_step(h)
-
-        @pl.loop(0, h)
-        def _(i):
-            meet(newest(h, 1), i, False)
+        for odd in range(2):
+            arrive(h, odd)
+            forward(h, odd).start()
+        for odd in range(2):
+            forward(h, odd).wait_recv()
+
+        @pl.loop(0, h // 2)
+        def _(k):
+            cross(h, 2 * k)
+            cross(h, 2 * k + 1)
+
+        @pl.loop(0, h % 2)
+        def _(k):
+            cross(h, h - 1)
 
         meet(whole(h), h, True)
 
@@ -233,10 +247,8 @@
     forward(last, 0).start()
     forward(last, 0).wait_recv()
 
-    @pl.loop(0, last)
-    def _(i):
+    for i in range(last):
         meet(newest(last, 0), i, False)
-
     arrive(last, 1)
     forward(last, 1).start()
     for j in range(last):
@@ -278,11 +290,10 @@
     nearest = pl.pallas_call(
         kernel,
         out_shape=jax.ShapeDtypeStruct((1, rows), jnp.float32),
-        in_specs=[pl.BlockSpec(memory_space=pltpu.HBM)] * 2,
+        in_specs=[pl.BlockSpec(memory_space=pltpu.HBM), pl.BlockSpec(memory_space=pltpu.VMEM)],
         out_specs=pl.BlockSpec(memory_space=pltpu.VMEM),
         scratch_shapes=[
             pltpu.VMEM((rows, features), jnp.bfloat16),
-            pltpu.VMEM((1, rows), jnp.int32),
             pltpu.VMEM((slots, features), jnp.bfloat16),
             pltpu.VMEM((2 * slots, features), jnp.bfloat16),
             pltpu.VMEM((8, slots), jnp.float32),
@@ -290,7 +301,8 @@
             pltpu.VMEM((CHIPS, 1, LANES), jnp.float32),
             pltpu.VMEM((CHIPS, rows), jnp.bfloat16),
             pltpu.SemaphoreType.DMA((4,)),
-            pltpu.SemaphoreType.DMA,
+            pltpu.SemaphoreType.REGULAR,
+            pltpu.SemaphoreType.REGULAR,
             pltpu.SemaphoreType.DMA,
             pltpu.SemaphoreType.DMA((PLANE,)),
             pltpu.SemaphoreType.DMA,
@@ -299,7 +311,7 @@
             pltpu.SemaphoreType.DMA,
         ],
         compiler_params=pltpu.CompilerParams(
-            collective_id=0, has_side_effects=True, vmem_limit_bytes=56 << 20
+            collective_id=0, has_side_effects=True, vmem_limit_bytes=53 << 20
         ),
         cost_estimate=pl.CostEstimate(
             flops=2 * slots * 2 * slots * features, bytes_accessed=2 * rows * features, transcendentals=0

time: 99.5 us -> 107 us (1.075)
  Pallas kernels: 98.1 us -> 106 us
    pallas_call x1, Pallas kernels: 98.1 us -> 106 us  [on_device(): pl.pallas_call(kernel, out_shape=jax.ShapeDtypeStruct((1, rows), jnp.floa...]
where the time goes in v4:
time: 107 us
  Pallas kernels  106 us (99%)
  local copies, waits for them, and re-layouts  1.28 us (1%)
    pallas_call x1, Pallas kernels, on_device(): pl.pallas_call(kernel, out_shape=jax.ShapeDtypeStruct((1, rows), jnp.floa...  106 us

profile of v4, /device:TPU:1, one launch (start us, length us, event | category | flops | bytes accessed | tf_op | source)
XLA Modules:
  0.0 106.8 jit_solution(13857057773714965272)
XLA Ops:
  0.0 0.0 copy-start
  0.0 0.7 copy-done
  0.7 105.5 %shard_map.28 = f32[1,1024]{1,0:T(1,128)S(1)} custom-call(bf16[1024,768]{1,0:T(8,128)(2,1)} %emb_hbm.1, s32[1,1024]{1,0:T(1,128)S(1)} %bitcast.3), custom_call_target="tpu_custom_call" | custom-call | flops 12884901888 | bytes 1572864 | tf_op jit(solution)/shard_map/pallas_call | solution.py:290
  106.2 0.6 copy.4
Async XLA Ops:
  0.0 0.7 copy-start

commit v5 on v4

--- a/solution.py
+++ b/solution.py
@@ -15,26 +15,20 @@
 BOTH = 2 * PAIR
 PAIRS = PLANE // 2
 EARLY = 2
-REACH = 3
+LOOPED = 6
+FAR_FIRST = (2, 0, 3, 4, 1, 5, 6)
 EMPTY = 4.0
 LOW = -1e30
 LANES = 128
 
 
-def hops(d, g):
-    p = PLANE - 1 - g
-    return sum(min(a, n - a) for a, n in ((d, NZ), (p // NY, NX), (p % NY, NY)))
-
-
-OFFSETS = [(d, g) for g in range(PLANE) for d in range(NZ) if hops(d, g)]
-NEAR = [o for o in OFFSETS if hops(*o) <= REACH]
-FAR = [o for o in OFFSETS if hops(*o) > REACH]
+OFFSETS = [(d, g) for g in range(PLANE) for d in range(NZ) if (d, g) != (0, PLANE - 1)]
 
 
 def kernel(
     emb_hbm, lab_ref, out_ref,
     emb, send, pool, acc, res, back, onehot,
-    emb_sem, near_sem, far_sem, send_sem, recv_sem, fwd_send, fwd_recv, ret_send, ret_recv,
+    emb_sem, send_sem, recv_sem, fwd_send, fwd_recv, ret_send, ret_recv,
 ):
     dp = lax.axis_index("dp")
     y = lax.axis_index("group")
@@ -67,17 +61,9 @@
 
     barrier = pltpu.get_barrier_semaphore()
 
-    def greet(d, g, counter):
-        chip, along = ahead(d, g)
-        pl.semaphore_signal(
-            barrier, inc=1, device_id=(chip - core + counter, along), device_id_type=MESH
-        )
-
+    for offset in OFFSETS:
+        pl.semaphore_signal(barrier, inc=1, device_id=ahead(*offset), device_id_type=MESH)
     pl.semaphore_signal(barrier, inc=1, device_id=sibling, device_id_type=MESH)
-    for offset in FAR:
-        greet(*offset, 1)
-    for offset in NEAR:
-        greet(*offset, 0)
 
     label = lab_ref[...]
     far_z = (label % NZ - z + NZ) % NZ
@@ -127,44 +113,21 @@
             device_id=ahead(d, g), device_id_type=MESH,
         )
 
-    def send_near(h):
-        for d, g in NEAR:
+    for h in range(EARLY):
+        dispatch(h)
+
+    pl.semaphore_wait(barrier, CHIPS)
+
+    for h in range(PAIRS):
+        if h >= EARLY:
+            dispatch(h)
+        if h == PAIRS - 1:
+            own_src = pl.ds((PLANE - 1) * GRP, CAP)
+            own_dst = pl.ds((PAIRS - 1) * BOTH + GRP, CAP)
+            pltpu.make_async_copy(send.at[own_src], pool.at[own_dst], recv_sem.at[PLANE - 1]).start()
+        for d, g in OFFSETS:
             if g // 2 == h:
                 outgoing(d, g).start()
-
-    for h in range(EARLY):
-        dispatch(h)
-
-    @pl.when(core == 0)
-    def _():
-        pl.semaphore_wait(barrier, 2 * len(NEAR) + 1)
-        pl.semaphore_signal(near_sem, inc=1, device_id=sibling, device_id_type=MESH)
-
-    @pl.when(core == 1)
-    def _():
-        pl.semaphore_wait(near_sem, 1)
-
-    for h in range(EARLY):
-        send_near(h)
-    for h in range(EARLY, PAIRS):
-        dispatch(h)
-        send_near(h)
-
-    own_src = pl.ds((PLANE - 1) * GRP, CAP)
-    own_dst = pl.ds((PAIRS - 1) * BOTH + GRP, CAP)
-    pltpu.make_async_copy(send.at[own_src], pool.at[own_dst], recv_sem.at[PLANE - 1]).start()
-
-    @pl.when(core == 1)
-    def _():
-        pl.semaphore_wait(barrier, 2 * len(FAR) + 1)
-        pl.semaphore_signal(far_sem, inc=1, device_id=sibling, device_id_type=MESH)
-
-    @pl.when(core == 0)
-    def _():
-        pl.semaphore_wait(far_sem, 1)
-
-    for d, g in FAR:
-        outgoing(d, g).start()
 
     def mine(h, odd):
         return pl.ds(pl.multiple_of(h * BOTH + odd * GRP, GRP), GRP)
@@ -205,7 +168,7 @@
         meet(whole(i), h, False)
         meet(whole(h), i, False)
 
-    @pl.loop(0, PAIRS - 1)
+    @pl.loop(0, LOOPED)
     def _(h):
         for odd in range(2):
             arrive(h, odd)
@@ -243,32 +206,35 @@
                 else:
                     returning(d, g).start()
 
-    arrive(last, 0)
-    forward(last, 0).start()
-    forward(last, 0).wait_recv()
-
-    for i in range(last):
-        meet(newest(last, 0), i, False)
-    arrive(last, 1)
-    forward(last, 1).start()
-    for j in range(last):
-        meet(whole(j), last, False)
-    forward(last, 1).wait_recv()
-    for i in range(last):
-        meet(newest(last, 1), i, False)
-        finish(i)
-    meet(whole(last), last, True)
-    finish(last)
+    def step(h, odd, then):
+        arrive(h, odd)
+        forward(h, odd).start()
+        if odd:
+            for j in range(h):
+                meet(whole(j), h, False)
+        forward(h, odd).wait_recv()
+        for i in FAR_FIRST:
+            if i < h:
+                meet(newest(h, odd), i, False)
+                then(i)
+        if odd:
+            meet(whole(h), h, True)
+            then(h)
+
+    for h in range(LOOPED, last):
+        step(h, 0, lambda i: None)
+        step(h, 1, lambda i: None)
+    step(last, 0, lambda i: None)
+    step(last, 1, finish)
 
     pltpu.make_async_copy(back, back, ret_recv).wait()
 
     got = back[...].reshape(CHIPS, LANES)
     high = got.astype(jnp.bfloat16)
     rest = got - high.astype(jnp.float32)
-    middle = rest.astype(jnp.bfloat16)
-    low = (rest - middle.astype(jnp.float32)).astype(jnp.bfloat16)
+    low = rest.astype(jnp.bfloat16)
     spread = jnp.zeros((LANES, rows), jnp.float32)
-    for part in (high, middle, low):
+    for part in (high, low):
         spread += lax.dot_general(
             part, onehot[...], (((0,), (0,)), ((), ())), preferred_element_type=jnp.float32
         )
@@ -301,8 +267,6 @@
             pltpu.VMEM((CHIPS, 1, LANES), jnp.float32),
             pltpu.VMEM((CHIPS, rows), jnp.bfloat16),
             pltpu.SemaphoreType.DMA((4,)),
-            pltpu.SemaphoreType.REGULAR,
-            pltpu.SemaphoreType.REGULAR,
             pltpu.SemaphoreType.DMA,
             pltpu.SemaphoreType.DMA((PLANE,)),
             pltpu.SemaphoreType.DMA,

time: 107 us -> 96 us (0.90)
  Pallas kernels: 106 us -> 94.6 us
    pallas_call x1, Pallas kernels: 106 us -> 94.6 us  [on_device(): pl.pallas_call(kernel, out_shape=jax.ShapeDtypeStruct((1, rows), jnp.floa...]
where the time goes in v5:
time: 96 us; the launch traced here: 95.9 us
  Pallas kernels  94.6 us (99%)
  local copies, waits for them, and re-layouts  1.28 us (1%)
    pallas_call x1, Pallas kernels, on_device(): pl.pallas_call(kernel, out_shape=jax.ShapeDtypeStruct((1, rows), jnp.floa...  94.6 us

profile of v5, /device:TPU:1, one launch (start us, length us, event | category | flops | bytes accessed | tf_op | source)
XLA Modules:
  0.0 95.9 jit_solution(12295595626112375247)
XLA Ops:
  0.0 0.0 copy-start
  0.0 0.7 copy-done
  0.7 94.6 %shard_map.28 = f32[1,1024]{1,0:T(1,128)S(1)} custom-call(bf16[1024,768]{1,0:T(8,128)(2,1)} %emb_hbm.1, s32[1,1024]{1,0:T(1,128)S(1)} %bitcast.3), custom_call_target="tpu_custom_call" | custom-call | flops 12884901888 | bytes 1572864 | tf_op jit(solution)/shard_map/pallas_call | solution.py:256
  95.3 0.6 copy.4
Async XLA Ops:
  0.0 0.7 copy-start

commit v6 on v5

--- a/solution.py
+++ b/solution.py
@@ -16,19 +16,44 @@
 PAIRS = PLANE // 2
 EARLY = 2
 LOOPED = 6
-FAR_FIRST = (2, 0, 3, 4, 1, 5, 6)
+BESIDE = 4
 EMPTY = 4.0
 LOW = -1e30
 LANES = 128
 
 
-OFFSETS = [(d, g) for g in range(PLANE) for d in range(NZ) if (d, g) != (0, PLANE - 1)]
+def steps(r):
+    p = PLANE - 1 - r // NZ
+    return r % NZ, p // NY, p % NY
+
+
+def hops(r):
+    return sum(min(a, n - a) for a, n in zip(steps(r), (NZ, NX, NY)))
+
+
+def arrange():
+    by_hops = sorted(range(CHIPS), key=lambda r: (hops(r), -r))
+    at = list(range(CHIPS))
+    for g, chosen in ((PLANE - 1, by_hops[:NZ]), (PLANE - 2, by_hops[NZ:2 * NZ])):
+        slots = range(g * NZ, (g + 1) * NZ)
+        coming = [r for r in chosen if at.index(r) not in slots]
+        for s in slots:
+            if at[s] not in chosen:
+                t = at.index(coming.pop())
+                at[s], at[t] = at[t], at[s]
+    return at
+
+
+AT = arrange()
+SELF = AT.index((PLANE - 1) * NZ)
+OTHERS = [s for s in range(CHIPS) if s != SELF]
+FAR_FIRST = sorted(range(PAIRS - 1), key=lambda i: -max(hops(r) for r in AT[2 * NZ * i:2 * NZ * (i + 1)]))
 
 
 def kernel(
-    emb_hbm, lab_ref, out_ref,
-    emb, send, pool, acc, res, back, onehot,
-    emb_sem, send_sem, recv_sem, fwd_send, fwd_recv, ret_send, ret_recv,
+    emb_hbm, lab_hbm, out_ref,
+    emb, lab, send, pool, acc, res, back, onehot,
+    emb_sem, lab_sem, send_sem, recv_sem, fwd_send, fwd_recv, ret_send, ret_recv,
 ):
     dp = lax.axis_index("dp")
     y = lax.axis_index("group")
@@ -40,6 +65,8 @@
         at = pl.ds(i * quarter, quarter)
         return pltpu.make_async_copy(emb_hbm.at[at], emb.at[at], emb_sem.at[i])
 
+    labels = pltpu.make_async_copy(lab_hbm, lab, lab_sem)
+    labels.start()
     for i in range(4):
         loading(i).start()
 
@@ -49,27 +76,32 @@
     x_ahead = [((x + d) % NX) * 2 for d in range(NX)]
     y_ahead = [(y + d) % NY for d in range(NY)]
 
-    def ahead(d, g):
-        p = PLANE - 1 - g
-        return (z_ahead[d] + x_ahead[p // NY], y_ahead[p % NY])
-
-    def behind(d, g):
-        p = PLANE - 1 - g
-        return (z_behind[d] + x_ahead[-(p // NY)], y_ahead[-(p % NY)])
+    def ahead(s):
+        dz, dx, dy = steps(AT[s])
+        return (z_ahead[dz] + x_ahead[dx], y_ahead[dy])
+
+    def behind(s):
+        dz, dx, dy = steps(AT[s])
+        return (z_behind[dz] + x_ahead[-dx], y_ahead[-dy])
 
     sibling = ((z * NX + x) * 2 + 1 - core, y)
 
     barrier = pltpu.get_barrier_semaphore()
 
-    for offset in OFFSETS:
-        pl.semaphore_signal(barrier, inc=1, device_id=ahead(*offset), device_id_type=MESH)
+    for s in OTHERS:
+        pl.semaphore_signal(barrier, inc=1, device_id=ahead(s), device_id_type=MESH)
     pl.semaphore_signal(barrier, inc=1, device_id=sibling, device_id_type=MESH)
 
-    label = lab_ref[...]
+    labels.wait()
+    label = lab[...]
     far_z = (label % NZ - z + NZ) % NZ
     far_x = (label // PLANE // 2 - x + NX) % NX
     far_y = ((label // NZ) % NY - y + NY) % NY
-    chip = (PLANE - 1 - far_x * NY - far_y) * NZ + far_z
+    offset = (PLANE - 1 - far_x * NY - far_y) * NZ + far_z
+    chip = offset
+    for s, r in enumerate(AT):
+        if s != r:
+            chip = jnp.where(offset == r, s, chip)
     hot = chip == lax.broadcasted_iota(jnp.int32, (CHIPS, rows), 0)
     ones = hot.astype(jnp.bfloat16)
     onehot[...] = ones
@@ -105,12 +137,14 @@
         send[pl.ds(base, PAIR), :LANES] = (wide[:, :LANES] + mark).astype(jnp.bfloat16)
         send[pl.ds(base, PAIR), LANES:] = wide[:, LANES:].astype(jnp.bfloat16)
 
-    def outgoing(d, g):
-        src = pl.ds(g * GRP + d * CAP, CAP)
-        dst = pl.ds((g // 2) * BOTH + (g % 2) * GRP + d * CAP, CAP)
+    def landing(s):
+        return pl.ds((s // (2 * NZ)) * BOTH + s % (2 * NZ) * CAP, CAP)
+
+    def outgoing(s):
+        src, dst = pl.ds(s * CAP, CAP), landing(s)
         return pltpu.make_async_remote_copy(
-            src_ref=send.at[src], dst_ref=pool.at[dst], send_sem=send_sem, recv_sem=recv_sem.at[g],
-            device_id=ahead(d, g), device_id_type=MESH,
+            src_ref=send.at[src], dst_ref=pool.at[dst], send_sem=send_sem, recv_sem=recv_sem.at[s // NZ],
+            device_id=ahead(s), device_id_type=MESH,
         )
 
     for h in range(EARLY):
@@ -121,13 +155,13 @@
     for h in range(PAIRS):
         if h >= EARLY:
             dispatch(h)
-        if h == PAIRS - 1:
-            own_src = pl.ds((PLANE - 1) * GRP, CAP)
-            own_dst = pl.ds((PAIRS - 1) * BOTH + GRP, CAP)
-            pltpu.make_async_copy(send.at[own_src], pool.at[own_dst], recv_sem.at[PLANE - 1]).start()
-        for d, g in OFFSETS:
-            if g // 2 == h:
-                outgoing(d, g).start()
+        for s in range(h * 2 * NZ, (h + 1) * 2 * NZ):
+            if s == SELF:
+                pltpu.make_async_copy(
+                    send.at[pl.ds(s * CAP, CAP)], pool.at[landing(s)], recv_sem.at[s // NZ]
+                ).start()
+            else:
+                outgoing(s).start()
 
     def mine(h, odd):
         return pl.ds(pl.multiple_of(h * BOTH + odd * GRP, GRP), GRP)
@@ -189,10 +223,10 @@
 
     last = PAIRS - 1
 
-    def returning(d, g):
+    def returning(s):
         return pltpu.make_async_remote_copy(
-            src_ref=res.at[g], dst_ref=back.at[g * NZ + d], send_sem=ret_send, recv_sem=ret_recv,
-            device_id=behind(d, g), device_id_type=MESH,
+            src_ref=res.at[s // NZ], dst_ref=back.at[s], send_sem=ret_send, recv_sem=ret_recv,
+            device_id=behind(s), device_id_type=MESH,
         )
 
     def finish(i):
@@ -200,17 +234,17 @@
         for odd in range(2):
             g = 2 * i + odd
             res[g] = best[:, odd * LANES:(odd + 1) * LANES]
-            for d in range(NZ):
-                if g == PLANE - 1 and d == 0:
-                    pltpu.make_async_copy(res.at[g], back.at[g * NZ], ret_recv).start()
+            for s in range(g * NZ, (g + 1) * NZ):
+                if s == SELF:
+                    pltpu.make_async_copy(res.at[g], back.at[s], ret_recv).start()
                 else:
-                    returning(d, g).start()
+                    returning(s).start()
 
     def step(h, odd, then):
         arrive(h, odd)
         forward(h, odd).start()
         if odd:
-            for j in range(h):
+            for j in range(min(h, BESIDE)):
                 meet(whole(j), h, False)
         forward(h, odd).wait_recv()
         for i in FAR_FIRST:
@@ -218,6 +252,8 @@
                 meet(newest(h, odd), i, False)
                 then(i)
         if odd:
+            for j in range(BESIDE, h):
+                meet(whole(j), h, False)
             meet(whole(h), h, True)
             then(h)
 
@@ -238,11 +274,11 @@
         spread += lax.dot_general(
             part, onehot[...], (((0,), (0,)), ((), ())), preferred_element_type=jnp.float32
         )
-    place = far_z * CAP + rank
+    place = (chip % NZ) * CAP + rank
     chosen = place == lax.broadcasted_iota(jnp.int32, (LANES, rows), 0)
     out_ref[...] = jnp.sum(jnp.where(chosen, spread, 0.0), axis=0, keepdims=True)
 
-    sent = pl.ds(CAP, (CHIPS - 1) * CAP)
+    sent = pl.ds(0, (CHIPS - 1) * CAP)
     pltpu.make_async_copy(send.at[sent], send.at[sent], send_sem).wait()
     half = pl.ds(0, PLANE * GRP)
     pltpu.make_async_copy(pool.at[half], pool.at[half], fwd_send).wait()
@@ -256,10 +292,11 @@
     nearest = pl.pallas_call(
         kernel,
         out_shape=jax.ShapeDtypeStruct((1, rows), jnp.float32),
-        in_specs=[pl.BlockSpec(memory_space=pltpu.HBM), pl.BlockSpec(memory_space=pltpu.VMEM)],
+        in_specs=[pl.BlockSpec(memory_space=pltpu.HBM)] * 2,
         out_specs=pl.BlockSpec(memory_space=pltpu.VMEM),
         scratch_shapes=[
             pltpu.VMEM((rows, features), jnp.bfloat16),
+            pltpu.VMEM((1, rows), jnp.int32),
             pltpu.VMEM((slots, features), jnp.bfloat16),
             pltpu.VMEM((2 * slots, features), jnp.bfloat16),
             pltpu.VMEM((8, slots), jnp.float32),
@@ -268,6 +305,7 @@
             pltpu.VMEM((CHIPS, rows), jnp.bfloat16),
             pltpu.SemaphoreType.DMA((4,)),
             pltpu.SemaphoreType.DMA,
+            pltpu.SemaphoreType.DMA,
             pltpu.SemaphoreType.DMA((PLANE,)),
             pltpu.SemaphoreType.DMA,
             pltpu.SemaphoreType.DMA((PLANE,)),
@@ -275,7 +313,7 @@
             pltpu.SemaphoreType.DMA,
         ],
         compiler_params=pltpu.CompilerParams(
-            collective_id=0, has_side_effects=True, vmem_limit_bytes=53 << 20
+            collective_id=0, has_side_effects=True, vmem_limit_bytes=55228 << 10
         ),
         cost_estimate=pl.CostEstimate(
             flops=2 * slots * 2 * slots * features, bytes_accessed=2 * rows * features, transcendentals=0

time: 96 us -> 99 us (1.031)
  Pallas kernels: 94.6 us -> 98.3 us
    pallas_call x1, Pallas kernels: 94.6 us -> 98.3 us  [on_device(): pl.pallas_call(kernel, out_shape=jax.ShapeDtypeStruct((1, rows), jnp.floa...]
where the time goes in v6:
time: 99 us; the launch traced here: 98.9 us
  Pallas kernels  98.3 us (99%)
    pallas_call x1, Pallas kernels, on_device(): pl.pallas_call(kernel, out_shape=jax.ShapeDtypeStruct((1, rows), jnp.floa...  98.3 us

profile of v6, /device:TPU:1, one launch (start us, length us, event | category | flops | bytes accessed | tf_op | source)
XLA Modules:
  0.0 98.9 jit_solution(11496872328712130288)
XLA Ops:
  0.0 98.3 %shard_map.28 = f32[1,1024]{1,0:T(1,128)S(1)} custom-call(bf16[1024,768]{1,0:T(8,128)(2,1)} %emb_hbm.1, s32[1,1024]{1,0:T(1,128)} %bitcast.3), custom_call_target="tpu_custom_call" | custom-call | flops 12884901888 | bytes 1572864 | tf_op jit(solution)/shard_map/pallas_call | solution.py:292
  98.3 0.6 copy.4

commit v7 on v6

--- a/solution.py
+++ b/solution.py
@@ -14,7 +14,7 @@
 PAIR = 2 * GRP
 BOTH = 2 * PAIR
 PAIRS = PLANE // 2
-EARLY = 2
+EARLY = 1
 LOOPED = 6
 BESIDE = 4
 EMPTY = 4.0
@@ -31,23 +31,9 @@
     return sum(min(a, n - a) for a, n in zip(steps(r), (NZ, NX, NY)))
 
 
-def arrange():
-    by_hops = sorted(range(CHIPS), key=lambda r: (hops(r), -r))
-    at = list(range(CHIPS))
-    for g, chosen in ((PLANE - 1, by_hops[:NZ]), (PLANE - 2, by_hops[NZ:2 * NZ])):
-        slots = range(g * NZ, (g + 1) * NZ)
-        coming = [r for r in chosen if at.index(r) not in slots]
-        for s in slots:
-            if at[s] not in chosen:
-                t = at.index(coming.pop())
-                at[s], at[t] = at[t], at[s]
-    return at
-
-
-AT = arrange()
-SELF = AT.index((PLANE - 1) * NZ)
+SELF = (PLANE - 1) * NZ
 OTHERS = [s for s in range(CHIPS) if s != SELF]
-FAR_FIRST = sorted(range(PAIRS - 1), key=lambda i: -max(hops(r) for r in AT[2 * NZ * i:2 * NZ * (i + 1)]))
+FAR_FIRST = sorted(range(PAIRS - 1), key=lambda i: -max(hops(s) for s in range(2 * NZ * i, 2 * NZ * (i + 1))))
 
 
 def kernel(
@@ -70,19 +56,18 @@
     for i in range(4):
         loading(i).start()
 
-    z_ahead = [((z + d) % NZ) * (2 * NX) + core for d in range(NZ)]
-    z_behind = [((z + NZ - d) % NZ) * (2 * NX) + core for d in range(NZ)]
-
-    x_ahead = [((x + d) % NX) * 2 for d in range(NX)]
-    y_ahead = [(y + d) % NY for d in range(NY)]
+    sign = 1 - 2 * core
+    z_ahead = [((z + sign * d + NZ) % NZ) * (2 * NX) + core for d in range(NZ)]
+    x_ahead = [((x + sign * d + NX) % NX) * 2 for d in range(NX)]
+    y_ahead = [(y + sign * d + NY) % NY for d in range(NY)]
 
     def ahead(s):
-        dz, dx, dy = steps(AT[s])
+        dz, dx, dy = steps(s)
         return (z_ahead[dz] + x_ahead[dx], y_ahead[dy])
 
     def behind(s):
-        dz, dx, dy = steps(AT[s])
-        return (z_behind[dz] + x_ahead[-dx], y_ahead[-dy])
+        dz, dx, dy = steps(s)
+        return (z_ahead[-dz] + x_ahead[-dx], y_ahead[-dy])
 
     sibling = ((z * NX + x) * 2 + 1 - core, y)
 
@@ -94,14 +79,10 @@
 
     labels.wait()
     label = lab[...]
-    far_z = (label % NZ - z + NZ) % NZ
-    far_x = (label // PLANE // 2 - x + NX) % NX
-    far_y = ((label // NZ) % NY - y + NY) % NY
-    offset = (PLANE - 1 - far_x * NY - far_y) * NZ + far_z
-    chip = offset
-    for s, r in enumerate(AT):
-        if s != r:
-            chip = jnp.where(offset == r, s, chip)
+    far_z = (sign * (label % NZ - z) + NZ) % NZ
+    far_x = (sign * (label // (NZ * NY) - x) + NX) % NX
+    far_y = (sign * ((label // NZ) % NY - y) + NY) % NY
+    chip = (PLANE - 1 - far_x * NY - far_y) * NZ + far_z
     hot = chip == lax.broadcasted_iota(jnp.int32, (CHIPS, rows), 0)
     ones = hot.astype(jnp.bfloat16)
     onehot[...] = ones
@@ -250,6 +231,8 @@
         for i in FAR_FIRST:
             if i < h:
                 meet(newest(h, odd), i, False)
+        for i in FAR_FIRST:
+            if i < h:
                 then(i)
         if odd:
             for j in range(BESIDE, h):
@@ -274,7 +257,7 @@
         spread += lax.dot_general(
             part, onehot[...], (((0,), (0,)), ((), ())), preferred_element_type=jnp.float32
         )
-    place = (chip % NZ) * CAP + rank
+    place = far_z * CAP + rank
     chosen = place == lax.broadcasted_iota(jnp.int32, (LANES, rows), 0)
     out_ref[...] = jnp.sum(jnp.where(chosen, spread, 0.0), axis=0, keepdims=True)
 

time: 99 us -> 94.1 us (0.951)
  Pallas kernels: 98.3 us -> 93.4 us
    pallas_call x1, Pallas kernels: 98.3 us -> 93.4 us  [on_device(): pl.pallas_call(kernel, out_shape=jax.ShapeDtypeStruct((1, rows), jnp.floa...]
where the time goes in v7:
time: 94.1 us; the launch traced here: 94 us
  Pallas kernels  93.4 us (99%)
    pallas_call x1, Pallas kernels, on_device(): pl.pallas_call(kernel, out_shape=jax.ShapeDtypeStruct((1, rows), jnp.floa...  93.4 us

profile of v7, /device:TPU:1, one launch (start us, length us, event | category | flops | bytes accessed | tf_op | source)
XLA Modules:
  0.0 94.0 jit_solution(4215496662318558357)
XLA Ops:
  0.0 93.4 %shard_map.28 = f32[1,1024]{1,0:T(1,128)S(1)} custom-call(bf16[1024,768]{1,0:T(8,128)(2,1)} %emb_hbm.1, s32[1,1024]{1,0:T(1,128)} %bitcast.3), custom_call_target="tpu_custom_call" | custom-call | flops 12884901888 | bytes 1572864 | tf_op jit(solution)/shard_map/pallas_call | solution.py:275
  93.4 0.6 copy.4

commit v8 on v7

--- a/solution.py
+++ b/solution.py
@@ -17,6 +17,7 @@
 EARLY = 1
 LOOPED = 6
 BESIDE = 4
+Z_ORDER = (4, 3, 5, 2, 6, 1, 7, 0)
 EMPTY = 4.0
 LOW = -1e30
 LANES = 128
@@ -85,7 +86,6 @@
     chip = (PLANE - 1 - far_x * NY - far_y) * NZ + far_z
     hot = chip == lax.broadcasted_iota(jnp.int32, (CHIPS, rows), 0)
     ones = hot.astype(jnp.bfloat16)
-    onehot[...] = ones
     row = lax.broadcasted_iota(jnp.int32, (LANES, 2 * LANES), 0)
     col = lax.broadcasted_iota(jnp.int32, (LANES, 2 * LANES), 1)
     before = ((row < col) | (col >= LANES)).astype(jnp.bfloat16)
@@ -136,13 +136,16 @@
     for h in range(PAIRS):
         if h >= EARLY:
             dispatch(h)
-        for s in range(h * 2 * NZ, (h + 1) * 2 * NZ):
+        for s in [(2 * h + odd) * NZ + d for odd in range(2) for d in Z_ORDER]:
             if s == SELF:
                 pltpu.make_async_copy(
                     send.at[pl.ds(s * CAP, CAP)], pool.at[landing(s)], recv_sem.at[s // NZ]
                 ).start()
             else:
                 outgoing(s).start()
+
+    onehot[:CHIPS] = ones
+    onehot[CHIPS:] = ones
 
     def mine(h, odd):
         return pl.ds(pl.multiple_of(h * BOTH + odd * GRP, GRP), GRP)
@@ -252,11 +255,10 @@
     high = got.astype(jnp.bfloat16)
     rest = got - high.astype(jnp.float32)
     low = rest.astype(jnp.bfloat16)
-    spread = jnp.zeros((LANES, rows), jnp.float32)
-    for part in (high, low):
-        spread += lax.dot_general(
-            part, onehot[...], (((0,), (0,)), ((), ())), preferred_element_type=jnp.float32
-        )
+    spread = lax.dot_general(
+        jnp.concatenate([high, low], axis=0), onehot[...], (((0,), (0,)), ((), ())),
+        preferred_element_type=jnp.float32,
+    )
     place = far_z * CAP + rank
     chosen = place == lax.broadcasted_iota(jnp.int32, (LANES, rows), 0)
     out_ref[...] = jnp.sum(jnp.where(chosen, spread, 0.0), axis=0, keepdims=True)
@@ -285,7 +287,7 @@
             pltpu.VMEM((8, slots), jnp.float32),
             pltpu.VMEM((PLANE, 1, LANES), jnp.float32),
             pltpu.VMEM((CHIPS, 1, LANES), jnp.float32),
-            pltpu.VMEM((CHIPS, rows), jnp.bfloat16),
+            pltpu.VMEM((2 * CHIPS, rows), jnp.bfloat16),
             pltpu.SemaphoreType.DMA((4,)),
             pltpu.SemaphoreType.DMA,
             pltpu.SemaphoreType.DMA,

time: 94.1 us -> 93.1 us (0.989)
  Pallas kernels: 93.4 us -> 92.4 us
    pallas_call x1, Pallas kernels: 93.4 us -> 92.4 us  [on_device(): pl.pallas_call(kernel, out_shape=jax.ShapeDtypeStruct((1, rows), jnp.floa...]
where the time goes in v8:
time: 93.1 us; the launch traced here: 93 us
  Pallas kernels  92.4 us (99%)
    pallas_call x1, Pallas kernels, on_device(): pl.pallas_call(kernel, out_shape=jax.ShapeDtypeStruct((1, rows), jnp.floa...  92.4 us

profile of v8, /device:TPU:1, one launch (start us, length us, event | category | flops | bytes accessed | tf_op | source)
XLA Modules:
  0.0 93.0 jit_solution(12899441919883583993)
XLA Ops:
  0.0 92.4 %shard_map.28 = f32[1,1024]{1,0:T(1,128)S(1)} custom-call(bf16[1024,768]{1,0:T(8,128)(2,1)} %emb_hbm.1, s32[1,1024]{1,0:T(1,128)} %bitcast.3), custom_call_target="tpu_custom_call" | custom-call | flops 12884901888 | bytes 1572864 | tf_op jit(solution)/shard_map/pallas_call | solution.py:277
  92.4 0.6 copy.4

commit v9 on v8

--- a/solution.py
+++ b/solution.py
@@ -17,7 +17,7 @@
 EARLY = 1
 LOOPED = 6
 BESIDE = 4
-Z_ORDER = (4, 3, 5, 2, 6, 1, 7, 0)
+LEAD = 0.25
 EMPTY = 4.0
 LOW = -1e30
 LANES = 128
@@ -33,8 +33,8 @@
 
 
 SELF = (PLANE - 1) * NZ
+SEND_ORDER = sorted(range(CHIPS), key=lambda s: (s // NZ - LEAD * min(s % NZ, NZ - s % NZ), s))
 OTHERS = [s for s in range(CHIPS) if s != SELF]
-FAR_FIRST = sorted(range(PAIRS - 1), key=lambda i: -max(hops(s) for s in range(2 * NZ * i, 2 * NZ * (i + 1))))
 
 
 def kernel(
@@ -74,7 +74,7 @@
 
     barrier = pltpu.get_barrier_semaphore()
 
-    for s in OTHERS:
+    for s in sorted(OTHERS, key=lambda s: -hops(s)):
         pl.semaphore_signal(barrier, inc=1, device_id=ahead(s), device_id_type=MESH)
     pl.semaphore_signal(barrier, inc=1, device_id=sibling, device_id_type=MESH)
 
@@ -133,16 +133,17 @@
 
     pl.semaphore_wait(barrier, CHIPS)
 
-    for h in range(PAIRS):
-        if h >= EARLY:
-            dispatch(h)
-        for s in [(2 * h + odd) * NZ + d for odd in range(2) for d in Z_ORDER]:
-            if s == SELF:
-                pltpu.make_async_copy(
-                    send.at[pl.ds(s * CAP, CAP)], pool.at[landing(s)], recv_sem.at[s // NZ]
-                ).start()
-            else:
-                outgoing(s).start()
+    ready = EARLY
+    for s in SEND_ORDER:
+        if s // (2 * NZ) == ready:
+            dispatch(ready)
+            ready += 1
+        if s == SELF:
+            pltpu.make_async_copy(
+                send.at[pl.ds(s * CAP, CAP)], pool.at[landing(s)], recv_sem.at[s // NZ]
+            ).start()
+        else:
+            outgoing(s).start()
 
     onehot[:CHIPS] = ones
     onehot[CHIPS:] = ones
@@ -213,16 +214,17 @@
             device_id=behind(s), device_id_type=MESH,
         )
 
-    def finish(i):
-        best = jnp.max(acc[:, i * PAIR:(i + 1) * PAIR], axis=0, keepdims=True)
-        for odd in range(2):
-            g = 2 * i + odd
-            res[g] = best[:, odd * LANES:(odd + 1) * LANES]
-            for s in range(g * NZ, (g + 1) * NZ):
-                if s == SELF:
-                    pltpu.make_async_copy(res.at[g], back.at[s], ret_recv).start()
-                else:
-                    returning(s).start()
+    def finish(pairs):
+        for i in pairs:
+            best = jnp.max(acc[:, i * PAIR:(i + 1) * PAIR], axis=0, keepdims=True)
+            for odd in range(2):
+                res[2 * i + odd] = best[:, odd * LANES:(odd + 1) * LANES]
+        slots = [s for i in pairs for s in range(2 * NZ * i, 2 * NZ * (i + 1))]
+        for s in sorted(slots, key=lambda s: -hops(s)):
+            if s == SELF:
+                pltpu.make_async_copy(res.at[s // NZ], back.at[s], ret_recv).start()
+            else:
+                returning(s).start()
 
     def step(h, odd, then):
         arrive(h, odd)
@@ -231,22 +233,19 @@
             for j in range(min(h, BESIDE)):
                 meet(whole(j), h, False)
         forward(h, odd).wait_recv()
-        for i in FAR_FIRST:
-            if i < h:
-                meet(newest(h, odd), i, False)
-        for i in FAR_FIRST:
-            if i < h:
-                then(i)
+        for i in range(h):
+            meet(newest(h, odd), i, False)
+        then(range(h))
         if odd:
             for j in range(BESIDE, h):
                 meet(whole(j), h, False)
             meet(whole(h), h, True)
-            then(h)
+            then([h])
 
     for h in range(LOOPED, last):
-        step(h, 0, lambda i: None)
-        step(h, 1, lambda i: None)
-    step(last, 0, lambda i: None)
+        step(h, 0, lambda pairs: None)
+        step(h, 1, lambda pairs: None)
+    step(last, 0, lambda pairs: None)
     step(last, 1, finish)
 
     pltpu.make_async_copy(back, back, ret_recv).wait()

time: 93.1 us -> 92.7 us (level)
  no operation moved by 1% of the time
where the time goes in v9:
time: 92.7 us; the launch traced here: 92.6 us
  Pallas kernels  92 us (99%)
    pallas_call x1, Pallas kernels, on_device(): pl.pallas_call(kernel, out_shape=jax.ShapeDtypeStruct((1, rows), jnp.floa...  92 us

profile of v9, /device:TPU:1, one launch (start us, length us, event | category | flops | bytes accessed | tf_op | source)
XLA Modules:
  0.0 92.6 jit_solution(12806730172238542991)
XLA Ops:
  0.0 92.0 %shard_map.28 = f32[1,1024]{1,0:T(1,128)S(1)} custom-call(bf16[1024,768]{1,0:T(8,128)(2,1)} %emb_hbm.1, s32[1,1024]{1,0:T(1,128)} %bitcast.3), custom_call_target="tpu_custom_call" | custom-call | flops 12884901888 | bytes 1572864 | tf_op jit(solution)/shard_map/pallas_call | solution.py:276
  92.0 0.6 copy.4

commit v10 on v9

--- a/solution.py
+++ b/solution.py
@@ -14,7 +14,6 @@
 PAIR = 2 * GRP
 BOTH = 2 * PAIR
 PAIRS = PLANE // 2
-EARLY = 1
 LOOPED = 6
 BESIDE = 4
 LEAD = 0.25
@@ -105,18 +104,17 @@
     for i in range(4):
         loading(i).wait()
 
-    def dispatch(h):
-        base = h * PAIR
-        pick = position == base + lax.broadcasted_iota(jnp.int32, (PAIR, rows), 0)
+    def dispatch(base, count):
+        pick = position == base + lax.broadcasted_iota(jnp.int32, (count, rows), 0)
         chosen = jnp.where(pick, 1.0, 0.0)
         filled = jnp.sum(chosen, axis=1, keepdims=True)
         wide = jnp.dot(chosen.astype(jnp.bfloat16), emb[...], preferred_element_type=jnp.float32)
         total = jnp.sum(wide * wide, axis=1, keepdims=True)
         wide = wide * (1.0 / jnp.sqrt(total + 1e-06))
-        lane = lax.broadcasted_iota(jnp.int32, (PAIR, LANES), 1)
+        lane = lax.broadcasted_iota(jnp.int32, (count, LANES), 1)
         mark = jnp.where((lane == 0) & (filled == 0.0), EMPTY, 0.0)
-        send[pl.ds(base, PAIR), :LANES] = (wide[:, :LANES] + mark).astype(jnp.bfloat16)
-        send[pl.ds(base, PAIR), LANES:] = wide[:, LANES:].astype(jnp.bfloat16)
+        send[pl.ds(base, count), :LANES] = (wide[:, :LANES] + mark).astype(jnp.bfloat16)
+        send[pl.ds(base, count), LANES:] = wide[:, LANES:].astype(jnp.bfloat16)
 
     def landing(s):
         return pl.ds((s // (2 * NZ)) * BOTH + s % (2 * NZ) * CAP, CAP)
@@ -128,16 +126,16 @@
             device_id=ahead(s), device_id_type=MESH,
         )
 
-    for h in range(EARLY):
-        dispatch(h)
+    dispatch(0, GRP)
 
     pl.semaphore_wait(barrier, CHIPS)
 
-    ready = EARLY
+    ready = GRP
     for s in SEND_ORDER:
-        if s // (2 * NZ) == ready:
-            dispatch(ready)
-            ready += 1
+        if s * CAP >= ready:
+            count = GRP if ready == GRP else PAIR
+            dispatch(ready, count)
+            ready += count
         if s == SELF:
             pltpu.make_async_copy(
                 send.at[pl.ds(s * CAP, CAP)], pool.at[landing(s)], recv_sem.at[s // NZ]

time: 92.7 us -> 92.7 us (level)
  no operation moved by 1% of the time
where the time goes in v10:
time: 92.7 us; the launch traced here: 92.6 us
  Pallas kernels  92 us (99%)
    pallas_call x1, Pallas kernels, on_device(): pl.pallas_call(kernel, out_shape=jax.ShapeDtypeStruct((1, rows), jnp.floa...  92 us

profile of v10, /device:TPU:1, one launch (start us, length us, event | category | flops | bytes accessed | tf_op | source)
XLA Modules:
  0.0 92.6 jit_solution(6652916356023649455)
XLA Ops:
  0.0 92.0 %shard_map.28 = f32[1,1024]{1,0:T(1,128)S(1)} custom-call(bf16[1024,768]{1,0:T(8,128)(2,1)} %emb_hbm.1, s32[1,1024]{1,0:T(1,128)} %bitcast.3), custom_call_target="tpu_custom_call" | custom-call | flops 12884901888 | bytes 1572864 | tf_op jit(solution)/shard_map/pallas_call | solution.py:274
  92.0 0.6 copy.4
